TPU v7x, 512 devices: a whole 4x8x8 slice. The times are simulated.
512 devices in a mesh: tm: 8 (over z), lon: 16 (over x_hi, y), lat: 4 (over x_lo, core).
Axes of the slice: x: 4 (x_hi: 2, x_lo: 2; x = x_hi * 2 + x_lo), y: 8, z: 8, core: 2. Of those that a mesh axis runs over, the one named last changes fastest.
Arguments:
- features: bfloat16 [16, 32, 1024, 128], P('tm', 'lat', 'lon'), may hold values from -6 to 6
- conv_first: bfloat16 [3, 3, 3, 128, 128], replicated, may hold values from -0.109375 to 0.109375
- conv_second: bfloat16 [3, 3, 3, 128, 128], replicated, may hold values from -0.109375 to 0.109375
Outputs:
- decoded: bfloat16 [16, 32, 1024, 128], P('tm', 'lat', 'lon')
All inputs are finite; a program needn't handle non-finite values.
Results may differ from a plain program's by a relative error of at most 0.003.
Values may be sent and summed in bfloat16 or wider, within the bound.
A program may use at most 64 MiB of HBM per device.

v0:
```python
import jax
import jax.numpy as jnp
from jax import lax
from jax.sharding import PartitionSpec as P


def extended(value, sides, width, wrap):
    for axis, dim in sides:
        peers, length = (lax.axis_size(axis), value.shape[dim])
        up = [(i, (i + 1) % peers) for i in range(peers if wrap else peers - 1)]
        down = [(j, i) for i, j in up]
        last = lax.slice_in_dim(value, length - width, length, axis=dim)
        first = lax.slice_in_dim(value, 0, width, axis=dim)
        before = lax.ppermute(last, axis, up)
        after = lax.ppermute(first, axis, down)
        value = jnp.concatenate([before, value, after], axis=dim)
    return value


def from_behind(value, axis, by):
    peers = lax.axis_size(axis)
    pairs = [(i, i + by) for i in range(peers) if 0 <= i + by < peers]
    return lax.ppermute(value, axis, pairs)


def extend(tiles):
    widened = extended(tiles, (("lon", 2),), 1, True)
    return extended(widened, (("lat", 1),), 1, False)


def causal_conv(padded, kernel):
    frames = padded.shape[0] - 2
    height = padded.shape[1] - 2
    breadth = padded.shape[2] - 2
    channels = padded.shape[3]
    summed = jnp.zeros((frames, height * breadth, kernel.shape[4]), jnp.float32)
    for row_tap in range(3):
        stripe = jnp.concatenate(
            [
                padded[:, row_tap : row_tap + height, col_tap : col_tap + breadth, :]
                for col_tap in range(3)
            ],
            axis=-1,
        )
        stripe = stripe.reshape(frames + 2, height * breadth, 3 * channels)
        for time_tap in range(3):
            taps = kernel[time_tap, row_tap].reshape(3 * channels, kernel.shape[4])
            summed = summed + jnp.einsum(
                "fpk,kc->fpc",
                stripe[time_tap : time_tap + frames],
                taps,
                preferred_element_type=jnp.float32,
            )
    return summed.reshape(frames, height, breadth, kernel.shape[4])


def local(features, conv_first, conv_second):
    earlier = from_behind(features, "tm", 1)
    stacked = jnp.concatenate([earlier, features], axis=0)
    stacked = extend(stacked)
    hidden = jax.nn.silu(causal_conv(stacked, conv_first)).astype(jnp.bfloat16)
    hidden_prev = from_behind(hidden, "tm", 1)
    hidden_ext = jnp.concatenate([hidden_prev, hidden], axis=0)
    hidden_ext = extend(hidden_ext)
    summed = features.astype(jnp.float32) + causal_conv(hidden_ext, conv_second)
    return summed.astype(jnp.bfloat16)


def solution(mesh):
    placed = (P("tm", "lat", "lon", None), P(), P())
    return jax.shard_map(
        local, mesh=mesh, in_specs=placed, out_specs=P("tm", "lat", "lon", None), check_vma=False
    )
```

profile of v0, /device:TPU:249, one launch (start us, length us, event | category | flops | bytes accessed | tf_op | source)
XLA Modules:
  0.0 73.8 jit_solution(11475287337306648753)
XLA Ops:
  0.0 5.3 %collective-permute-start = (bf16[2,8,64,128]{3,2,1,0:T(8,128)(2,1)}, bf16[2,8,64,128]{3,2,1,0:T(8,128)(2,1)S(1)}, u32[]{:S(2)}, u32[]{:S(2)}) collective-permute-start(bf16[2,8,64,128]{3,2,1,0:T(8,128)(2,1)} %param.3), channel_id=1, source_target_pairs={{0,64},{64,128},{128,192},{192,256},{256,320},{320,384},{384,448},... | collective-permute-start | bytes 786440 | tf_op jit(solution)/shard_map/ppermute | solution.py:23
  5.3 5.3 %collective-permute-done = bf16[2,8,64,128]{3,2,1,0:T(8,128)(2,1)S(1)} collective-permute-done((bf16[2,8,64,128]{3,2,1,0:T(8,128)(2,1)}, bf16[2,8,64,128]{3,2,1,0:T(8,128)(2,1)S(1)}, u32[]{:S(2)}, u32[]{:S(2)}) %collective-permute-start) | collective-permute-done | bytes 262176 | tf_op jit(solution)/shard_map/ppermute | solution.py:23
  10.6 1.0 %constant_dynamic-update-slice_fusion = bf16[4,8,64,128]{3,2,1,0:T(8,128)(2,1)S(1)} fusion(bf16[4,8,64,128]{3,2,1,0:T(8,128)(2,1)S(1)} %constant_dynamic-update-slice_fusion.1, bf16[2,8,64,128]{3,2,1,0:T(8,128)(2,1)} %param.3), kind=kLoop, calls=%fused_computation.45 | loop fusion | bytes 524288 | tf_op jit(solution)/shard_map/concatenate | solution.py:59
  11.7 3.9 %collective-permute-start.1 = (bf16[4,8,1,128]{3,2,1,0:T(2,128)(2,1)S(1)}, bf16[4,8,1,128]{3,2,1,0:T(2,128)(2,1)S(1)}, u32[]{:S(2)}, u32[]{:S(2)}) collective-permute-start(bf16[4,8,1,128]{3,2,1,0:T(2,128)(2,1)S(1)} %get-tuple-element.63), channel_id=1, source_target_pairs={{0,4},{4,8},{8,12},{12,16},{16,20},{20,24},{24,28},{28,32},{32,36}... | collective-permute-start | bytes 24584 | tf_op jit(solution)/shard_map/ppermute | solution.py:14
  15.5 1.9 %collective-permute-start.2 = (bf16[4,8,1,128]{3,2,1,0:T(2,128)(2,1)S(1)}, bf16[4,8,1,128]{3,2,1,0:T(2,128)(2,1)S(1)}, u32[]{:S(2)}, u32[]{:S(2)}) collective-permute-start(bf16[4,8,1,128]{3,2,1,0:T(2,128)(2,1)S(1)} %get-tuple-element.64), channel_id=1, source_target_pairs={{4,0},{8,4},{12,8},{16,12},{20,16},{24,20},{28,24},{32,28},{36,32}... | collective-permute-start | bytes 24584 | tf_op jit(solution)/shard_map/ppermute | solution.py:15
  17.6 6.1 %collective-permute-done.2 = bf16[4,8,1,128]{3,2,1,0:T(2,128)(2,1)S(1)} collective-permute-done((bf16[4,8,1,128]{3,2,1,0:T(2,128)(2,1)S(1)}, bf16[4,8,1,128]{3,2,1,0:T(2,128)(2,1)S(1)}, u32[]{:S(2)}, u32[]{:S(2)}) %collective-permute-start.2) | collective-permute-done | bytes 8224 | tf_op jit(solution)/shard_map/ppermute | solution.py:15
  23.7 5.1 %collective-permute-start.3 = (bf16[4,1,66,128]{3,2,1,0:T(8,128)(2,1)S(1)}, bf16[4,1,66,128]{3,2,1,0:T(8,128)(2,1)S(1)}, u32[]{:S(2)}, u32[]{:S(2)}) collective-permute-start(bf16[4,1,66,128]{3,2,1,0:T(8,128)(2,1)S(1)} %get-tuple-element.59), channel_id=1, source_target_pairs={{0,1},{1,2},{2,3},{4,5},{5,6},{6,7},{8,9},{9,10},{10,11},{12,13},{... | collective-permute-start | bytes 202760 | tf_op jit(solution)/shard_map/ppermute | solution.py:14
  28.8 1.9 %collective-permute-start.4 = (bf16[4,1,66,128]{3,2,1,0:T(8,128)(2,1)S(1)}, bf16[4,1,66,128]{3,2,1,0:T(8,128)(2,1)S(1)}, u32[]{:S(2)}, u32[]{:S(2)}) collective-permute-start(bf16[4,1,66,128]{3,2,1,0:T(8,128)(2,1)S(1)} %get-tuple-element.60), channel_id=1, source_target_pairs={{1,0},{2,1},{3,2},{5,4},{6,5},{7,6},{9,8},{10,9},{11,10},{13,12},{... | collective-permute-start | bytes 202760 | tf_op jit(solution)/shard_map/ppermute | solution.py:15
  30.7 0.6 fusion.2
  31.6 0.4 fusion.24
  32.0 0.4 fusion.25
  32.4 2.1 %collective-permute-done.4 = bf16[4,1,66,128]{3,2,1,0:T(8,128)(2,1)S(1)} collective-permute-done((bf16[4,1,66,128]{3,2,1,0:T(8,128)(2,1)S(1)}, bf16[4,1,66,128]{3,2,1,0:T(8,128)(2,1)S(1)}, u32[]{:S(2)}, u32[]{:S(2)}) %collective-permute-start.4) | collective-permute-done | bytes 67616 | tf_op jit(solution)/shard_map/ppermute | solution.py:15
  34.4 0.3 maximum_maximum_fusion
  34.8 0.7 fusion.20
  35.7 0.3 fusion.15
  36.3 0.3 fusion.13
  36.6 0.4 fusion.23
  36.9 0.4 fusion.26
  37.3 0.4 convolution_add_fusion.9
  37.7 0.4 convolution_add_fusion.8
  38.1 0.4 fusion.8
  38.5 0.4 convolution_add_fusion.6
  38.9 0.4 convolution_add_fusion.5
  39.4 5.2 %collective-permute-start.5 = (bf16[2,8,64,128]{3,2,1,0:T(8,128)(2,1)S(1)}, bf16[2,8,64,128]{3,2,1,0:T(8,128)(2,1)S(1)}, u32[]{:S(2)}, u32[]{:S(2)}) collective-permute-start(bf16[2,8,64,128]{3,2,1,0:T(8,128)(2,1)S(1)} %multiply_convert_fusion), channel_id=1, source_target_pairs={{0,64},{64,128},{128,192},{192,256},{256,320},{320,384},{384,448},... | collective-permute-start | bytes 786440 | tf_op jit(solution)/shard_map/ppermute | solution.py:23
  44.6 4.1 %collective-permute-done.5 = bf16[2,8,64,128]{3,2,1,0:T(8,128)(2,1)S(1)} collective-permute-done((bf16[2,8,64,128]{3,2,1,0:T(8,128)(2,1)S(1)}, bf16[2,8,64,128]{3,2,1,0:T(8,128)(2,1)S(1)}, u32[]{:S(2)}, u32[]{:S(2)}) %collective-permute-start.5) | collective-permute-done | bytes 262176 | tf_op jit(solution)/shard_map/ppermute | solution.py:23
  48.7 2.0 %collective-permute-start.6 = (bf16[4,8,1,128]{3,2,1,0:T(2,128)(2,1)S(1)}, bf16[4,8,1,128]{3,2,1,0:T(2,128)(2,1)S(1)}, u32[]{:S(2)}, u32[]{:S(2)}) collective-permute-start(bf16[4,8,1,128]{3,2,1,0:T(2,128)(2,1)S(1)} %get-tuple-element.61), channel_id=1, source_target_pairs={{0,4},{4,8},{8,12},{12,16},{16,20},{20,24},{24,28},{28,32},{32,36}... | collective-permute-start | bytes 24584 | tf_op jit(solution)/shard_map/ppermute | solution.py:14
  50.7 3.3 %collective-permute-start.7 = (bf16[4,8,1,128]{3,2,1,0:T(2,128)(2,1)S(1)}, bf16[4,8,1,128]{3,2,1,0:T(2,128)(2,1)S(1)}, u32[]{:S(2)}, u32[]{:S(2)}) collective-permute-start(bf16[4,8,1,128]{3,2,1,0:T(2,128)(2,1)S(1)} %get-tuple-element.62), channel_id=1, source_target_pairs={{4,0},{8,4},{12,8},{16,12},{20,16},{24,20},{28,24},{32,28},{36,32}... | collective-permute-start | bytes 24584 | tf_op jit(solution)/shard_map/ppermute | solution.py:15
  54.1 4.7 %collective-permute-done.7 = bf16[4,8,1,128]{3,2,1,0:T(2,128)(2,1)S(1)} collective-permute-done((bf16[4,8,1,128]{3,2,1,0:T(2,128)(2,1)S(1)}, bf16[4,8,1,128]{3,2,1,0:T(2,128)(2,1)S(1)}, u32[]{:S(2)}, u32[]{:S(2)}) %collective-permute-start.7) | collective-permute-done | bytes 8224 | tf_op jit(solution)/shard_map/ppermute | solution.py:15
  58.9 3.4 %collective-permute-start.8 = (bf16[4,1,66,128]{3,2,1,0:T(8,128)(2,1)S(1)}, bf16[4,1,66,128]{3,2,1,0:T(8,128)(2,1)S(1)}, u32[]{:S(2)}, u32[]{:S(2)}) collective-permute-start(bf16[4,1,66,128]{3,2,1,0:T(8,128)(2,1)S(1)} %get-tuple-element.55), channel_id=1, source_target_pairs={{0,1},{1,2},{2,3},{4,5},{5,6},{6,7},{8,9},{9,10},{10,11},{12,13},{... | collective-permute-start | bytes 202760 | tf_op jit(solution)/shard_map/ppermute | solution.py:14
  62.3 1.9 %collective-permute-start.9 = (bf16[4,1,66,128]{3,2,1,0:T(8,128)(2,1)S(1)}, bf16[4,1,66,128]{3,2,1,0:T(8,128)(2,1)S(1)}, u32[]{:S(2)}, u32[]{:S(2)}) collective-permute-start(bf16[4,1,66,128]{3,2,1,0:T(8,128)(2,1)S(1)} %get-tuple-element.56), channel_id=1, source_target_pairs={{1,0},{2,1},{3,2},{5,4},{6,5},{7,6},{9,8},{10,9},{11,10},{13,12},{... | collective-permute-start | bytes 202760 | tf_op jit(solution)/shard_map/ppermute | solution.py:15
  64.2 0.7 fusion
  64.9 0.4 fusion.11
  65.3 0.4 fusion.28
  65.7 0.4 fusion.29
  66.0 1.9 %collective-permute-done.9 = bf16[4,1,66,128]{3,2,1,0:T(8,128)(2,1)S(1)} collective-permute-done((bf16[4,1,66,128]{3,2,1,0:T(8,128)(2,1)S(1)}, bf16[4,1,66,128]{3,2,1,0:T(8,128)(2,1)S(1)}, u32[]{:S(2)}, u32[]{:S(2)}) %collective-permute-start.9) | collective-permute-done | bytes 67616 | tf_op jit(solution)/shard_map/ppermute | solution.py:15
  67.9 0.3 maximum_maximum_fusion.1
  68.3 0.3 fusion.18
  68.8 0.4 fusion.12
  69.2 0.4 fusion.19
  69.8 0.3 fusion.10
  70.2 0.4 fusion.27
  70.5 0.4 fusion.30
  70.9 0.4 convolution_add_fusion.4
  71.3 0.4 convolution_add_fusion.3
  71.6 0.4 fusion.9
  72.0 0.4 convolution_add_fusion.1
  72.4 0.4 convolution_add_fusion
  73.0 0.8 %add_convert_fusion = bf16[2,8,64,128]{3,2,1,0:T(8,128)(2,1)} fusion(f32[2,8,64,128]{3,2,1,0:T(8,128)S(1)} %bitcast.129, bf16[2,8,64,128]{3,2,1,0:T(8,128)(2,1)S(1)} %copy-done), kind=kLoop, calls=%fused_computation.34 | loop fusion | flops 393216 | bytes 1048576 | tf_op jit(solution)/shard_map/convert_element_type | solution.py:66
  (23 shorter events, 1.9 us)
Async XLA Ops:
  0.0 17.5 %copy-start.1 = (bf16[3,3,3,128,128]{4,3,2,1,0:T(8,128)(2,1)S(1)}, bf16[3,3,3,128,128]{4,3,2,1,0:T(8,128)(2,1)}, u32[]{:S(2)}) copy-start(bf16[3,3,3,128,128]{4,3,2,1,0:T(8,128)(2,1)} %param.4) | copy-start | bytes 2654212
  0.0 10.6 %collective-permute-start = (bf16[2,8,64,128]{3,2,1,0:T(8,128)(2,1)}, bf16[2,8,64,128]{3,2,1,0:T(8,128)(2,1)S(1)}, u32[]{:S(2)}, u32[]{:S(2)}) collective-permute-start(bf16[2,8,64,128]{3,2,1,0:T(8,128)(2,1)} %param.3), channel_id=1, source_target_pairs={{0,64},{64,128},{128,192},{192,256},{256,320},{320,384},{384,448},... | collective-permute-start | bytes 786440 | tf_op jit(solution)/shard_map/ppermute | solution.py:23
  11.7 5.9 %collective-permute-start.1 = (bf16[4,8,1,128]{3,2,1,0:T(2,128)(2,1)S(1)}, bf16[4,8,1,128]{3,2,1,0:T(2,128)(2,1)S(1)}, u32[]{:S(2)}, u32[]{:S(2)}) collective-permute-start(bf16[4,8,1,128]{3,2,1,0:T(2,128)(2,1)S(1)} %get-tuple-element.63), channel_id=1, source_target_pairs={{0,4},{4,8},{8,12},{12,16},{16,20},{20,24},{24,28},{28,32},{32,36}... | collective-permute-start | bytes 24584 | tf_op jit(solution)/shard_map/ppermute | solution.py:14
  15.5 8.1 %collective-permute-start.2 = (bf16[4,8,1,128]{3,2,1,0:T(2,128)(2,1)S(1)}, bf16[4,8,1,128]{3,2,1,0:T(2,128)(2,1)S(1)}, u32[]{:S(2)}, u32[]{:S(2)}) collective-permute-start(bf16[4,8,1,128]{3,2,1,0:T(2,128)(2,1)S(1)} %get-tuple-element.64), channel_id=1, source_target_pairs={{4,0},{8,4},{12,8},{16,12},{20,16},{24,20},{28,24},{32,28},{36,32}... | collective-permute-start | bytes 24584 | tf_op jit(solution)/shard_map/ppermute | solution.py:15
  23.7 8.7 %collective-permute-start.3 = (bf16[4,1,66,128]{3,2,1,0:T(8,128)(2,1)S(1)}, bf16[4,1,66,128]{3,2,1,0:T(8,128)(2,1)S(1)}, u32[]{:S(2)}, u32[]{:S(2)}) collective-permute-start(bf16[4,1,66,128]{3,2,1,0:T(8,128)(2,1)S(1)} %get-tuple-element.59), channel_id=1, source_target_pairs={{0,1},{1,2},{2,3},{4,5},{5,6},{6,7},{8,9},{9,10},{10,11},{12,13},{... | collective-permute-start | bytes 202760 | tf_op jit(solution)/shard_map/ppermute | solution.py:14
  28.8 5.7 %collective-permute-start.4 = (bf16[4,1,66,128]{3,2,1,0:T(8,128)(2,1)S(1)}, bf16[4,1,66,128]{3,2,1,0:T(8,128)(2,1)S(1)}, u32[]{:S(2)}, u32[]{:S(2)}) collective-permute-start(bf16[4,1,66,128]{3,2,1,0:T(8,128)(2,1)S(1)} %get-tuple-element.60), channel_id=1, source_target_pairs={{1,0},{2,1},{3,2},{5,4},{6,5},{7,6},{9,8},{10,9},{11,10},{13,12},{... | collective-permute-start | bytes 202760 | tf_op jit(solution)/shard_map/ppermute | solution.py:15
  38.9 15.2 %copy-start.2 = (bf16[3,3,3,128,128]{4,3,2,1,0:T(8,128)(2,1)S(1)}, bf16[3,3,3,128,128]{4,3,2,1,0:T(8,128)(2,1)}, u32[]{:S(2)}) copy-start(bf16[3,3,3,128,128]{4,3,2,1,0:T(8,128)(2,1)} %param.5) | copy-start | bytes 2654212
  39.4 9.3 %collective-permute-start.5 = (bf16[2,8,64,128]{3,2,1,0:T(8,128)(2,1)S(1)}, bf16[2,8,64,128]{3,2,1,0:T(8,128)(2,1)S(1)}, u32[]{:S(2)}, u32[]{:S(2)}) collective-permute-start(bf16[2,8,64,128]{3,2,1,0:T(8,128)(2,1)S(1)} %multiply_convert_fusion), channel_id=1, source_target_pairs={{0,64},{64,128},{128,192},{192,256},{256,320},{320,384},{384,448},... | collective-permute-start | bytes 786440 | tf_op jit(solution)/shard_map/ppermute | solution.py:23
  48.7 5.4 %collective-permute-start.6 = (bf16[4,8,1,128]{3,2,1,0:T(2,128)(2,1)S(1)}, bf16[4,8,1,128]{3,2,1,0:T(2,128)(2,1)S(1)}, u32[]{:S(2)}, u32[]{:S(2)}) collective-permute-start(bf16[4,8,1,128]{3,2,1,0:T(2,128)(2,1)S(1)} %get-tuple-element.61), channel_id=1, source_target_pairs={{0,4},{4,8},{8,12},{12,16},{16,20},{20,24},{24,28},{28,32},{32,36}... | collective-permute-start | bytes 24584 | tf_op jit(solution)/shard_map/ppermute | solution.py:14
  50.7 8.1 %collective-permute-start.7 = (bf16[4,8,1,128]{3,2,1,0:T(2,128)(2,1)S(1)}, bf16[4,8,1,128]{3,2,1,0:T(2,128)(2,1)S(1)}, u32[]{:S(2)}, u32[]{:S(2)}) collective-permute-start(bf16[4,8,1,128]{3,2,1,0:T(2,128)(2,1)S(1)} %get-tuple-element.62), channel_id=1, source_target_pairs={{4,0},{8,4},{12,8},{16,12},{20,16},{24,20},{28,24},{32,28},{36,32}... | collective-permute-start | bytes 24584 | tf_op jit(solution)/shard_map/ppermute | solution.py:15
  58.9 7.2 %collective-permute-start.8 = (bf16[4,1,66,128]{3,2,1,0:T(8,128)(2,1)S(1)}, bf16[4,1,66,128]{3,2,1,0:T(8,128)(2,1)S(1)}, u32[]{:S(2)}, u32[]{:S(2)}) collective-permute-start(bf16[4,1,66,128]{3,2,1,0:T(8,128)(2,1)S(1)} %get-tuple-element.55), channel_id=1, source_target_pairs={{0,1},{1,2},{2,3},{4,5},{5,6},{6,7},{8,9},{9,10},{10,11},{12,13},{... | collective-permute-start | bytes 202760 | tf_op jit(solution)/shard_map/ppermute | solution.py:14
  62.3 5.7 %collective-permute-start.9 = (bf16[4,1,66,128]{3,2,1,0:T(8,128)(2,1)S(1)}, bf16[4,1,66,128]{3,2,1,0:T(8,128)(2,1)S(1)}, u32[]{:S(2)}, u32[]{:S(2)}) collective-permute-start(bf16[4,1,66,128]{3,2,1,0:T(8,128)(2,1)S(1)} %get-tuple-element.56), channel_id=1, source_target_pairs={{1,0},{2,1},{3,2},{5,4},{6,5},{7,6},{9,8},{10,9},{11,10},{13,12},{... | collective-permute-start | bytes 202760 | tf_op jit(solution)/shard_map/ppermute | solution.py:15
  72.0 1.0 %copy-start = (bf16[2,8,64,128]{3,2,1,0:T(8,128)(2,1)S(1)}, bf16[2,8,64,128]{3,2,1,0:T(8,128)(2,1)}, u32[]{:S(2)}) copy-start(bf16[2,8,64,128]{3,2,1,0:T(8,128)(2,1)} %param.3) | copy-start | bytes 786436
where the time goes:
time: 74.3 us; the launch traced here: 73.8 us
  starting transfers between devices  33.9 us (46%)
  waiting for transfers between devices  24 us (32%)
  matrix products  6.64 us (9%)
  local copies, waits for them, and re-layouts  4.76 us (6%)
  other arithmetic  3.94 us (5%)
    ppermute x4, waiting for transfers between devices, extended(): after = lax.ppermute(first, axis, down)  14.7 us
    ppermute x4, starting transfers between devices, extended(): before = lax.ppermute(last, axis, up)  14.3 us
    ppermute x2, starting transfers between devices, from_behind(): return lax.ppermute(value, axis, pairs)  10.5 us
    ppermute x2, waiting for transfers between devices, from_behind(): return lax.ppermute(value, axis, pairs)  9.34 us
    ppermute x4, starting transfers between devices, extended(): after = lax.ppermute(first, axis, down)  9.08 us
    dot_general x18, matrix products, causal_conv(): jnp.einsum('fpk,kc->fpc', stripe[time_tap:time_tap + frames], taps, prefe...  6.64 us
    concatenate x6, other arithmetic, causal_conv(): jnp.concatenate([padded[:, row_tap:row_tap + height, col_tap:col_tap + br...  2.24 us
    slice x6, local copies, waits for them, and re-layouts, causal_conv(): stripe[time_tap:time_tap + frames]  1.95 us
  transfers between devices with their start and end apart: 10, of which 6 were waited for; matrix products, arithmetic and copies ran while one was open for 5% of the time, Pallas kernels for 0%

commit v1 on v0

v1 whole, which is shorter than its diff:
```python
import jax
import jax.numpy as jnp
from jax import lax
from jax.experimental import pallas as pl
from jax.experimental.pallas import tpu as pltpu
from jax.sharding import PartitionSpec as P

MESH = pl.DeviceIdType.MESH
BF16, F32 = jnp.bfloat16, jnp.float32
F0P, F1P, F0, F1, H0P, H1P, H0, H1 = range(8)
NEXT = {F0: F0P, F1: F1P, H0: H0P, H1: H1P}


def block(groups, tiles_lon, tiles_lat, f_ref, k1_ref, k2_ref, o_ref, xc, xl, xr, pack, rim, w1, w2, acc, out,
          zsend, zrecv, lsend, lrecv, load, store):
    tm, lon, lat = lax.axis_index("tm"), lax.axis_index("lon"), lax.axis_index("lat")
    rows, cols, chan = f_ref.shape[1:]
    spots = rows * cols
    east, west = lax.rem(lon + 1, tiles_lon), lax.rem(lon + tiles_lon - 1, tiles_lon)
    has_prev, has_next, has_up, has_down = tm > 0, tm < groups - 1, lat > 0, lat < tiles_lat - 1

    barrier = pltpu.get_barrier_semaphore()

    def greet(**device):
        pl.semaphore_signal(barrier, inc=1, device_id=device, device_id_type=MESH)

    greet(lon=east)
    greet(lon=west)

    @pl.when(has_prev)
    def _():
        greet(tm=tm - 1)

    @pl.when(has_up)
    def _():
        for to in (lon, east, west):
            greet(lat=lat - 1, lon=to)

    @pl.when(has_down)
    def _():
        for to in (lon, east, west):
            greet(lat=lat + 1, lon=to)

    loads = [
        pltpu.make_async_copy(f_ref.at[1], xc.at[F1, pl.ds(1, rows)], load.at[0]),
        pltpu.make_async_copy(f_ref.at[0], xc.at[F0, pl.ds(1, rows)], load.at[1]),
        pltpu.make_async_copy(k1_ref, w1, load.at[2]),
        pltpu.make_async_copy(k2_ref, w2, load.at[3]),
    ]
    for copy in loads:
        copy.start()

    @pl.when(jnp.logical_not(has_prev))
    def _():
        for s in (F0P, F1P, H0P, H1P):
            xc[s] = jnp.zeros(xc.shape[1:], BF16)
            rim[s] = jnp.zeros(rim.shape[1:], BF16)

    @pl.when(jnp.logical_not(has_up))
    def _():
        for s in range(8):
            xc[s, 0] = jnp.zeros((cols, chan), BF16)
            rim[s, 2:4] = jnp.zeros((2, 16, chan), BF16)

    @pl.when(jnp.logical_not(has_down))
    def _():
        for s in range(8):
            xc[s, rows + 1] = jnp.zeros((cols, chan), BF16)
            rim[s, 4:6] = jnp.zeros((2, 16, chan), BF16)

    def remote(src, dst, sems, i, **device):
        return lambda: pltpu.make_async_remote_copy(
            src_ref=src, dst_ref=dst, send_sem=sems[0].at[i], recv_sem=sems[1].at[i],
            device_id=device, device_id_type=MESH)

    def forward(s):
        d, z = NEXT[s], (zsend, zrecv)
        i = 4 * (d if d < F0 else d - 2)
        to = lax.rem(tm + 1, groups)
        inner = pl.ds(2, rows - 2)
        return [
            remote(pack.at[s], pack.at[d], z, i, tm=to),
            remote(xc.at[s, 1], xc.at[d, 1], z, i + 1, tm=to),
            remote(xc.at[s, rows], xc.at[d, rows], z, i + 2, tm=to),
            remote(xc.at[s, inner], xc.at[d, inner], z, i + 3, tm=to),
        ]

    def sideways(s):
        z, i = (lsend, lrecv), 8 * s
        up, down = lax.rem(lat + tiles_lat - 1, tiles_lat), lax.rem(lat + 1, tiles_lat)
        return (
            [
                remote(pack.at[s], rim.at[s, 0], z, i, lon=east),
                remote(pack.at[s], rim.at[s, 1], z, i + 1, lon=west),
            ],
            [
                remote(xc.at[s, 1], xc.at[s, rows + 1], z, i + 2, lat=up),
                remote(pack.at[s], rim.at[s, 4], z, i + 3, lat=up, lon=east),
                remote(pack.at[s], rim.at[s, 5], z, i + 4, lat=up, lon=west),
            ],
            [
                remote(xc.at[s, rows], xc.at[s, 0], z, i + 5, lat=down),
                remote(pack.at[s], rim.at[s, 2], z, i + 6, lat=down, lon=east),
                remote(pack.at[s], rim.at[s, 3], z, i + 7, lat=down, lon=west),
            ],
        )

    def when_past(s, run):
        if s in (F0P, F1P, H0P, H1P):
            pl.when(has_prev)(run)
        else:
            run()

    def each(copies, method):
        for copy in copies:
            getattr(copy(), method)()

    def spread(s, method):
        def run():
            along, above, below = sideways(s)
            sent = method != "wait_recv"
            each(along, method)
            pl.when(has_up if sent else has_down)(lambda: each(above, method))
            pl.when(has_down if sent else has_up)(lambda: each(below, method))
        when_past(s, run)

    def send_on(s, method):
        pl.when(has_next)(lambda: each(forward(s), method))

    def edges_in(s):
        def run():
            each(forward(s)[:3], "wait_recv")
        pl.when(has_prev)(run)
        spread(NEXT[s], "start")

    def inner_in(s):
        pl.when(has_prev)(lambda: each(forward(s)[3:], "wait_recv"))

    def pack_of(x):
        return jnp.concatenate([x[r, j:j + 1] for j in (0, cols - 1) for r in range(rows)], axis=0)

    def shift(s):
        spread(s, "wait_recv")
        for r in range(rows + 2):
            if r == 0:
                left, right = rim[s, 2, 2 * rows - 1:], rim[s, 3, rows - 1:rows]
            elif r == rows + 1:
                left, right = rim[s, 4, rows:rows + 1], rim[s, 5, 0:1]
            else:
                left, right = rim[s, 0, rows + r - 1:rows + r], rim[s, 1, r - 1:r]
            x = xc[s, r]
            xl[s, r] = jnp.concatenate([left, x[:cols - 1]], axis=0)
            xr[s, r] = jnp.concatenate([x[1:], right], axis=0)

    def taps(s, w, times):
        left = jnp.concatenate(
            [ref[s, b:b + rows].reshape(spots, chan) for b in range(3) for ref in (xl, xc, xr)], axis=1)
        right = jnp.concatenate([w[a].reshape(9 * chan, chan) for a in times], axis=1)
        return jnp.dot(left, right, preferred_element_type=F32)

    def silu(v):
        return (v / (1 + jnp.exp(-v))).astype(BF16)

    def make_hidden(s, v):
        h = silu(v).reshape(rows, cols, chan)
        xc[s, 1:rows + 1] = h
        pack[s] = pack_of(h)
        send_on(s, "start")
        spread(s, "start")

    for s, copy in ((F1, loads[0]), (F0, loads[1])):
        copy.wait()
        pack[s] = pack_of(xc[s, 1:rows + 1])
    pl.semaphore_wait(
        barrier, 2 + has_next.astype(jnp.int32) + 3 * has_up.astype(jnp.int32) + 3 * has_down.astype(jnp.int32))

    for s in (F1, F0):
        send_on(s, "start")
    for s in (F1, F0):
        spread(s, "start")
    loads[2].wait()
    edges_in(F1)
    shift(F1)
    acc[:, chan:] = taps(F1, w1, (2,))
    shift(F0)
    v = taps(F0, w1, (2, 1))
    acc[:, :chan] = v[:, :chan]
    acc[:, chan:] += v[:, chan:]
    edges_in(F0)
    inner_in(F1)
    shift(F1P)
    v = acc[...] + taps(F1P, w1, (1, 0))
    acc[:, :chan] = v[:, :chan]
    make_hidden(H1, v[:, chan:])
    inner_in(F0)
    shift(F0P)
    make_hidden(H0, acc[:, :chan] + taps(F0P, w1, (0,)))

    loads[3].wait()
    edges_in(H1)
    shift(H1)
    acc[:, chan:] = xc[F1, 1:rows + 1].reshape(spots, chan).astype(F32) + taps(H1, w2, (2,))
    edges_in(H0)
    shift(H0)
    v = taps(H0, w2, (2, 1))
    acc[:, :chan] = xc[F0, 1:rows + 1].reshape(spots, chan).astype(F32) + v[:, :chan]
    acc[:, chan:] += v[:, chan:]
    for s in (F1, F0, H1, H0):
        send_on(s, "wait_send")
    for s in (F1, F0, F1P, F0P, H1, H0, H1P):
        spread(s, "wait_send")
    inner_in(H1)
    shift(H1P)
    v = acc[...] + taps(H1P, w2, (1, 0))
    acc[:, :chan] = v[:, :chan]
    out[1] = v[:, chan:].astype(BF16).reshape(rows, cols, chan)
    stores = [pltpu.make_async_copy(out.at[t], o_ref.at[t], store.at[t]) for t in range(2)]
    stores[1].start()
    inner_in(H0)
    shift(H0P)
    out[0] = (acc[:, :chan] + taps(H0P, w2, (0,))).astype(BF16).reshape(rows, cols, chan)
    stores[0].start()
    spread(H0P, "wait_send")
    for copy in stores:
        copy.wait()


def solution(mesh):
    groups, tiles_lon, tiles_lat = mesh.shape["tm"], mesh.shape["lon"], mesh.shape["lat"]

    def local(features, conv_first, conv_second):
        frames, rows, cols, chan = features.shape
        frame = (8, rows + 2, cols, chan)

        def kernel(*refs):
            block(groups, tiles_lon, tiles_lat, *refs)

        return pl.pallas_call(
            kernel,
            out_shape=jax.ShapeDtypeStruct(features.shape, BF16),
            in_specs=[pl.BlockSpec(memory_space=pl.ANY)] * 3,
            out_specs=pl.BlockSpec(memory_space=pl.ANY),
            scratch_shapes=[
                pltpu.VMEM(frame, BF16),
                pltpu.VMEM(frame, BF16),
                pltpu.VMEM(frame, BF16),
                pltpu.VMEM((8, 2 * rows, chan), BF16),
                pltpu.VMEM((8, 6, 2 * rows, chan), BF16),
                pltpu.VMEM(conv_first.shape, BF16),
                pltpu.VMEM(conv_second.shape, BF16),
                pltpu.VMEM((rows * cols, 2 * chan), F32),
                pltpu.VMEM(features.shape, BF16),
                pltpu.SemaphoreType.DMA((16,)),
                pltpu.SemaphoreType.DMA((16,)),
                pltpu.SemaphoreType.DMA((64,)),
                pltpu.SemaphoreType.DMA((64,)),
                pltpu.SemaphoreType.DMA((4,)),
                pltpu.SemaphoreType.DMA((2,)),
            ],
            compiler_params=pltpu.CompilerParams(
                collective_id=0, has_side_effects=True, vmem_limit_bytes=32 * 2**20),
            cost_estimate=pl.CostEstimate(flops=2 * 2 * 1024 * 27 * chan * chan, bytes_accessed=3 * 2**20, transcendentals=2**17),
            name="conv_block",
        )(features, conv_first, conv_second)

    placed = P("tm", "lat", "lon", None)
    return jax.shard_map(local, mesh=mesh, in_specs=(placed, P(), P()), out_specs=placed, check_vma=False)
```

time: 74.3 us -> 32.6 us (0.44)
  the two profiles are of different devices: /device:TPU:249 before, /device:TPU:65 now
where the time goes in v1:
time: 32.6 us; the launch traced here: 32.4 us
  Pallas kernels  28.4 us (87%)
  local copies, waits for them, and re-layouts  3.99 us (12%)
    pallas_call x1, Pallas kernels, local(): pl.pallas_call(kernel, out_shape=jax.ShapeDtypeStruct(features.shape, BF1...  28.4 us
    unnamed x7, local copies, waits for them, and re-layouts  3.99 us

profile of v1, /device:TPU:65, one launch (start us, length us, event | category | flops | bytes accessed | tf_op | source)
XLA Modules:
  0.0 32.4 jit_solution(2768027052684421514)
XLA Ops:
  0.0 0.0 copy-start
  0.0 1.2 %copy-done = bf16[3,3,3,128,128]{4,3,2,1,0:T(8,128)(2,1)S(1)} copy-done((bf16[3,3,3,128,128]{4,3,2,1,0:T(8,128)(2,1)S(1)}, bf16[3,3,3,128,128]{4,3,2,1,0:T(8,128)(2,1)}, u32[]{:S(2)}) %copy-start) | copy-done | bytes 884760
  1.2 0.0 copy-start.1
  1.2 1.2 %copy-done.1 = bf16[3,3,3,128,128]{4,3,2,1,0:T(8,128)(2,1)S(1)} copy-done((bf16[3,3,3,128,128]{4,3,2,1,0:T(8,128)(2,1)S(1)}, bf16[3,3,3,128,128]{4,3,2,1,0:T(8,128)(2,1)}, u32[]{:S(2)}) %copy-start.1) | copy-done | bytes 884760
  2.3 0.0 copy-start.2
  2.3 0.9 %copy-done.2 = bf16[2,8,64,128]{3,2,1,0:T(8,128)(2,1)S(1)} copy-done((bf16[2,8,64,128]{3,2,1,0:T(8,128)(2,1)S(1)}, bf16[2,8,64,128]{3,2,1,0:T(8,128)(2,1)}, u32[]{:S(2)}) %copy-start.2) | copy-done | bytes 262168
  3.3 28.4 %conv_block.1 = bf16[2,8,64,128]{3,2,1,0:T(8,128)(2,1)S(1)} custom-call(bf16[2,8,64,128]{3,2,1,0:T(8,128)(2,1)S(1)} %copy-done.2, bf16[3,3,3,128,128]{4,3,2,1,0:T(8,128)(2,1)S(1)} %copy-done, bf16[3,3,3,128,128]{4,3,2,1,0:T(8,128)(2,1)S(1)} %copy-done.1), custom_call_target="tpu_custom_call" | custom-call | flops 1811939328 | bytes 3145728 | tf_op jit(solution)/shard_map/conv_block/pallas_call | solution.py:238
  31.7 0.7 %copy.5 = bf16[2,8,64,128]{3,2,1,0:T(8,128)(2,1)} copy(bf16[2,8,64,128]{3,2,1,0:T(8,128)(2,1)S(1)} %conv_block.1) | data formatting | bytes 524288
Async XLA Ops:
  0.0 1.2 %copy-start = (bf16[3,3,3,128,128]{4,3,2,1,0:T(8,128)(2,1)S(1)}, bf16[3,3,3,128,128]{4,3,2,1,0:T(8,128)(2,1)}, u32[]{:S(2)}) copy-start(bf16[3,3,3,128,128]{4,3,2,1,0:T(8,128)(2,1)} %refs_1_.1) | copy-start | bytes 2654212
  1.2 1.2 %copy-start.1 = (bf16[3,3,3,128,128]{4,3,2,1,0:T(8,128)(2,1)S(1)}, bf16[3,3,3,128,128]{4,3,2,1,0:T(8,128)(2,1)}, u32[]{:S(2)}) copy-start(bf16[3,3,3,128,128]{4,3,2,1,0:T(8,128)(2,1)} %refs_2_.1) | copy-start | bytes 2654212
  2.3 0.9 %copy-start.2 = (bf16[2,8,64,128]{3,2,1,0:T(8,128)(2,1)S(1)}, bf16[2,8,64,128]{3,2,1,0:T(8,128)(2,1)}, u32[]{:S(2)}) copy-start(bf16[2,8,64,128]{3,2,1,0:T(8,128)(2,1)} %refs_0_.1) | copy-start | bytes 786436

commit v2 on v0

v2 whole, which is shorter than its diff:
```python
import jax
import jax.numpy as jnp
from jax import lax
from jax.experimental import pallas as pl
from jax.experimental.pallas import tpu as pltpu
from jax.sharding import PartitionSpec as P

MESH = pl.DeviceIdType.MESH
BF16, F32, I32 = jnp.bfloat16, jnp.float32, jnp.int32
F0P, F1P, F0, F1, H0P, H1P, H0, H1 = range(8)
NEXT = {F0: F0P, F1: F1P, H0: H0P, H1: H1P}
E, W, U, UE, UW, D, DE, DW = range(8)
STEP = {E: (1, 0), W: (-1, 0), U: (0, -1), UE: (1, -1), UW: (-1, -1), D: (0, 1), DE: (1, 1), DW: (-1, 1)}
BACK = {E: W, W: E, U: D, D: U, UE: DW, DW: UE, UW: DE, DE: UW}
RIM = {E: 0, W: 1, DE: 2, DW: 3, UE: 4, UW: 5}
T = 16


def block(groups, tiles_lon, tiles_lat, f_ref, k1_ref, k2_ref, o_ref, xc, xl, xr, pack, rim, halo, w1, w2,
          acc_in, acc_out, acc, zsend, zrecv, lsend, lrecv, load, entered):
    tm, lon, lat = lax.axis_index("tm"), lax.axis_index("lon"), lax.axis_index("lat")
    rows, cols, chan = f_ref.shape[1:]
    has_prev, has_next, has_up, has_down = tm > 0, tm < groups - 1, lat > 0, lat < tiles_lat - 1

    ring = tiles_lon // 2

    def lateness(at):
        y = lax.rem(at, ring)
        return jnp.minimum(y, ring - y)

    east, west = lax.rem(lon + 1, tiles_lon), lax.rem(lon + tiles_lon - 1, tiles_lon)
    earlier_e, earlier_w = lateness(east) < lateness(lon), lateness(west) < lateness(lon)
    later_e, later_w = jnp.logical_not(earlier_e), jnp.logical_not(earlier_w)
    far_e, far_w = lax.rem(lon, ring) == ring - 1, lax.rem(lon, ring) == 0
    near_e, near_w = jnp.logical_not(far_e), jnp.logical_not(far_w)
    far = jnp.logical_or(far_e, far_w)
    up, down = lax.rem(lat + tiles_lat - 1, tiles_lat), lax.rem(lat + 1, tiles_lat)

    def device(d):
        step_lon, step_lat = STEP[d]
        to = {}
        if step_lon:
            to["lon"] = east if step_lon > 0 else west
        if step_lat:
            to["lat"] = down if step_lat > 0 else up
        return to

    def toward(ds, *runs):
        def some(rise):
            return [d for d in ds if STEP[d][1] == rise]

        def all_of(ds):
            for run in runs:
                for d in ds:
                    run(d)

        all_of(some(0))
        for rise, cond in ((-1, has_up), (1, has_down)):
            if some(rise):
                pl.when(cond)(lambda rise=rise: all_of(some(rise)))

    barrier = pltpu.get_barrier_semaphore()

    def greet(d):
        pl.semaphore_signal(barrier, inc=1, device_id=device(d), device_id_type=MESH)

    @pl.when(has_prev)
    def _():
        pl.semaphore_signal(barrier, inc=1, device_id={"tm": tm - 1}, device_id_type=MESH)

    toward((U, D, W), greet)
    pl.when(near_e)(lambda: greet(E))
    pl.when(later_e)(lambda: toward((UE, DE), greet))
    pl.when(later_w)(lambda: toward((UW, DW), greet))

    loads = [
        pltpu.make_async_copy(f_ref.at[1], xc.at[F1, pl.ds(1, rows)], load.at[0]),
        pltpu.make_async_copy(f_ref.at[0], xc.at[F0, pl.ds(1, rows)], load.at[1]),
        pltpu.make_async_copy(k1_ref, w1, load.at[2]),
        pltpu.make_async_copy(k2_ref, w2, load.at[3]),
    ]
    for copy in loads:
        copy.start()

    def remote(src, dst, sems, i, to):
        return pltpu.make_async_remote_copy(
            src_ref=src, dst_ref=dst, send_sem=sems[0].at[i], recv_sem=sems[1].at[i], device_id=to, device_id_type=MESH)

    body, both, past = pl.ds(1, rows), pl.ds(F0, 2), pl.ds(F0P, 2)
    left, inner, right = pl.ds(0, T), pl.ds(T, cols - 2 * T), pl.ds(cols - T, T)

    PACKS, F1_TOP, F1_LOW, F1_MID, F0_TOP, F0_LOW, F0_MID = range(7)
    H1_HALO, H1_IN, H1_LEFT, H1_RIGHT, H0_HALO, H0_TOP, H0_LOW, H0_MID = range(7, 15)

    def forward(i):
        def at(s, *where):
            return xc.at[(s, *where)], xc.at[(NEXT[s], *where)]

        mid = pl.ds(2, rows - 2)
        src, dst = {
            PACKS: lambda: (pack.at[both], pack.at[past]),
            F1_TOP: lambda: at(F1, 1), F1_LOW: lambda: at(F1, rows), F1_MID: lambda: at(F1, mid),
            F0_TOP: lambda: at(F0, 1), F0_LOW: lambda: at(F0, rows), F0_MID: lambda: at(F0, mid),
            H1_HALO: lambda: (halo.at[H1 - 4, 0], halo.at[H1P - 4, 0]),
            H1_IN: lambda: at(H1, body, inner), H1_LEFT: lambda: at(H1, body, left), H1_RIGHT: lambda: at(H1, body, right),
            H0_HALO: lambda: (halo.at[H0 - 4, 0], halo.at[H0P - 4, 0]),
            H0_TOP: lambda: at(H0, 1), H0_LOW: lambda: at(H0, rows), H0_MID: lambda: at(H0, mid),
        }[i]()
        return remote(src, dst, (zsend, zrecv), i, {"tm": lax.rem(tm + 1, groups)})

    def send_on(*parts):
        pl.when(has_next)(lambda: [forward(p).start() for p in parts] and None)

    def arrived(*parts):
        pl.when(has_prev)(lambda: [forward(p).wait_recv() for p in parts] and None)

    def own(d):
        if d in RIM:
            src, dst = pack.at[both, int(STEP[d][0] > 0)], rim.at[both, RIM[d]]
        else:
            src, dst = xc.at[both, 1 if d == U else rows], xc.at[both, rows + 1 if d == U else 0]
        return remote(src, dst, (lsend, lrecv), d, device(d))

    def past_pack(d):
        return remote(pack.at[past, int(STEP[d][0] > 0)], rim.at[past, RIM[d]], (lsend, lrecv), 8 + d, device(d))

    def row(s):
        base = {F1P: 8, F0P: 16}.get(s, 24 + 4 * (s - 4))

        def make(d):
            return remote(
                xc.at[s, 1 if d == U else rows], xc.at[s, rows + 1 if d == U else 0],
                (lsend, lrecv), base + (d if s < H0P else int(d == D)), device(d))
        return make

    def halo_of(s):
        def make(d):
            return remote(
                halo.at[s - 4, 0], halo.at[s - 4, 2 if d == U else 1],
                (lsend, lrecv), 26 + 4 * (s - 4) + int(d == D), device(d))
        return make

    def send(*makes):
        return [lambda d, make=make: make(d).start() for make in makes]

    def receive(*makes):
        return [lambda d, make=make: make(BACK[d]).wait_recv() for make in makes]

    def sent(*makes):
        return [lambda d, make=make: make(d).wait_send() for make in makes]

    def if_past(run):
        pl.when(has_prev)(run)

    ROWS, SIDES = (U, D), (E, UE, DE, W, UW, DW)

    @pl.when(jnp.logical_not(has_prev))
    def _():
        for s in (F0P, F1P, H0P, H1P):
            xc[s] = jnp.zeros(xc.shape[1:], BF16)
        pack[past] = jnp.zeros((2, *pack.shape[1:]), BF16)
        rim[past] = jnp.zeros((2, *rim.shape[1:]), BF16)
        halo[0:2] = jnp.zeros((2, *halo.shape[1:]), BF16)

    @pl.when(jnp.logical_not(has_up))
    def _():
        for s in range(8):
            xc[s, 0] = jnp.zeros((cols, chan), BF16)
        for s in range(4):
            rim[s, 2:4] = jnp.zeros((2, 2 * rows, chan), BF16)
            halo[s, 1] = jnp.zeros((2 * rows, chan), BF16)

    @pl.when(jnp.logical_not(has_down))
    def _():
        for s in range(8):
            xc[s, rows + 1] = jnp.zeros((cols, chan), BF16)
        for s in range(4):
            rim[s, 4:6] = jnp.zeros((2, 2 * rows, chan), BF16)
            halo[s, 2] = jnp.zeros((2 * rows, chan), BF16)

    def make_pack(s):
        for half, at in ((0, 0), (1, cols - T)):
            tile = [xc[s, r, at:at + T] for r in range(1, rows + 1)]
            js = (0, 1) if half == 0 else (T - 2, T - 1)
            pack[s, half] = jnp.concatenate([x[j:j + 1] for j in js for x in tile], axis=0)

    def beside(s, r):
        if s < H0P:
            if r == 0:
                return rim[s, 2, 2 * rows - 1:], rim[s, 3, rows - 1:rows]
            if r == rows + 1:
                return rim[s, 4, rows:rows + 1], rim[s, 5, 0:1]
            return rim[s, 0, rows + r - 1:rows + r], rim[s, 1, r - 1:r]
        if r == 0:
            return halo[s - 4, 1, rows - 1:rows], halo[s - 4, 1, 2 * rows - 1:]
        if r == rows + 1:
            return halo[s - 4, 2, 0:1], halo[s - 4, 2, rows:rows + 1]
        return halo[s - 4, 0, r - 1:r], halo[s - 4, 0, rows + r - 1:rows + r]

    def shift_in(s):
        for r in range(rows + 2):
            x = xc[s, r]
            xl[s, r, T:cols - T] = x[T - 1:cols - T - 1]
            xr[s, r, T:cols - T] = x[T + 1:cols - T + 1]

    def shift_out(s):
        for r in range(rows + 2):
            before, after = beside(s, r)
            x = xc[s, r]
            xl[s, r, 0:T] = jnp.concatenate([before, x[:T - 1]], axis=0)
            xl[s, r, cols - T:] = x[cols - T - 1:cols - 1]
            xr[s, r, 0:T] = x[1:T + 1]
            xr[s, r, cols - T:] = jnp.concatenate([x[cols - T + 1:], after], axis=0)

    def shift_all(s):
        for r in range(rows + 2):
            before, after = beside(s, r)
            x = xc[s, r]
            xl[s, r] = jnp.concatenate([before, x[:cols - 1]], axis=0)
            xr[s, r] = jnp.concatenate([x[1:], after], axis=0)

    def halo_taps(s):
        def column(above, mid, below):
            above, mid, below = above.astype(F32), mid.astype(F32), below.astype(F32)
            return (jnp.concatenate([above, mid[:rows - 1]], axis=0), mid, jnp.concatenate([mid[1:], below], axis=0))

        def rim_column(at, side):
            k = side
            return column(rim[s, k + 2, at + rows - 1:at + rows], rim[s, k, at:at + rows], rim[s, k + 4, at:at + 1])

        first = column(xc[s, 0, 0:1], pack[s, 0, 0:rows], xc[s, rows + 1, 0:1])
        last = column(xc[s, 0, cols - 1:], pack[s, 1, rows:], xc[s, rows + 1, cols - 1:])
        wests = (rim_column(0, 0), rim_column(rows, 0), first)
        easts = (last, rim_column(0, 1), rim_column(rows, 1))
        return jnp.concatenate(
            [jnp.concatenate([wests[c][b], easts[c][b]], axis=0).astype(BF16) for b in range(3) for c in range(3)], axis=1)

    IN, OUT, ALL = (slice(T, cols - T),), (slice(0, T), slice(cols - T, cols)), (slice(0, cols),)

    def taken(ref, s, b, cuts):
        some = [ref[s, b:b + rows, c] for c in cuts]
        some = some[0] if len(some) == 1 else jnp.concatenate(some, axis=1)
        return some.reshape(-1, chan)

    def taps(s, w, times, cuts):
        x = jnp.concatenate([taken(ref, s, b, cuts) for b in range(3) for ref in (xl, xc, xr)], axis=1)
        if cuts is OUT:
            x = jnp.concatenate([x, halo_taps(s)], axis=0)
        k = jnp.concatenate([w[a].reshape(9 * chan, chan) for a in times], axis=1)
        return jnp.dot(x, k, preferred_element_type=F32)

    def shift(s, cuts):
        (shift_in if cuts is IN else shift_out if cuts is OUT else shift_all)(s)

    def own_frames(later, earlier, w, acc, cuts):
        shift(later, cuts)
        shift(earlier, cuts)
        v = taps(earlier, w, (2, 1), cuts)
        acc[:, :chan] = v[:, :chan]
        acc[:, chan:] = v[:, chan:] + taps(later, w, (2,), cuts)

    def past_later(s, w, acc, cuts):
        shift(s, cuts)
        v = acc[...] + taps(s, w, (1, 0), cuts)
        acc[:, :chan] = v[:, :chan]
        return v[:, chan:]

    def past_earlier(s, w, acc, cuts):
        shift(s, cuts)
        return acc[:, :chan] + taps(s, w, (0,), cuts)

    def silu(v):
        return (v / (1 + jnp.exp(-v))).astype(BF16)

    def hidden_in(s, v):
        xc[s, 1:rows + 1, T:cols - T] = silu(v).reshape(rows, cols - 2 * T, chan)

    def hidden_out(s, v):
        h = silu(v)
        halo[s - 4, 0] = h[2 * T * rows:]
        h = h[:2 * T * rows].reshape(rows, 2 * T, chan)
        xc[s, 1:rows + 1, 0:T] = h[:, :T]
        xc[s, 1:rows + 1, cols - T:] = h[:, T:]

    def result(t, v):
        x = xc[(F0, F1)[t], 1:rows + 1].reshape(-1, chan).astype(F32) + v
        o_ref[t] = x.astype(BF16).reshape(rows, cols, chan)

    for s, copy in ((F1, loads[0]), (F0, loads[1])):
        copy.wait()
        make_pack(s)

    heights = has_up.astype(I32) + has_down.astype(I32)
    pl.semaphore_wait(
        barrier,
        1 + has_next.astype(I32) + near_w.astype(I32) + heights * (1 + earlier_e.astype(I32) + earlier_w.astype(I32)))

    send_on(PACKS, F1_TOP, F1_LOW, F1_MID, F0_TOP, F0_LOW, F0_MID)

    def tell(d):
        pl.semaphore_signal(entered.at[BACK[d]], inc=1, device_id=device(d), device_id_type=MESH)

    def told(d):
        pl.semaphore_wait(entered.at[d], 1)

    pl.when(far_e)(lambda: tell(E))
    pl.when(earlier_e)(lambda: toward((UE, DE), tell))
    pl.when(earlier_w)(lambda: toward((UW, DW), tell))

    def known(*runs, rows=()):
        toward((E, *rows), *runs)
        pl.when(near_w)(lambda: toward((W,), *runs))
        pl.when(earlier_e)(lambda: toward((UE, DE), *runs))
        pl.when(earlier_w)(lambda: toward((UW, DW), *runs))

    def send_past_pack(d):
        if_past(lambda: past_pack(d).start())

    def after_word(ds):
        toward(ds, told, *send(own), send_past_pack)

    known(*send(own), rows=ROWS)
    arrived(PACKS)
    if_past(lambda: known(*send(past_pack)))
    arrived(F1_TOP, F1_LOW)
    if_past(lambda: toward(ROWS, *send(row(F1P))))
    loads[2].wait()
    toward(ROWS, *receive(own))
    own_frames(F1, F0, w1, acc_in, IN)
    pl.when(later_e)(lambda: after_word((UE, DE)))
    pl.when(jnp.logical_and(later_w, near_w))(lambda: after_word((UW, DW)))
    arrived(F1_MID)
    if_past(lambda: toward(ROWS, *receive(row(F1P))))
    hidden_in(H1, past_later(F1P, w1, acc_in, IN))
    send_on(H1_IN)
    arrived(F0_TOP, F0_LOW)
    if_past(lambda: toward(ROWS, *send(row(F0P))))
    pl.when(far_w)(lambda: after_word((W, UW, DW)))

    def outer_later():
        toward(SIDES, *receive(own))
        own_frames(F1, F0, w1, acc_out, OUT)
        if_past(lambda: toward(SIDES, *receive(past_pack)))
        hidden_out(H1, past_later(F1P, w1, acc_out, OUT))
        send_on(H1_HALO, H1_LEFT, H1_RIGHT)
        toward(ROWS, *send(row(H1), halo_of(H1)))

    pl.when(jnp.logical_not(far))(outer_later)
    arrived(F0_MID)
    if_past(lambda: toward(ROWS, *receive(row(F0P))))
    hidden_in(H0, past_earlier(F0P, w1, acc_in, IN))
    pl.when(far)(outer_later)
    hidden_out(H0, past_earlier(F0P, w1, acc_out, OUT))
    send_on(H0_HALO, H0_TOP, H0_LOW, H0_MID)
    toward(ROWS, *send(row(H0), halo_of(H0)))

    loads[3].wait()
    arrived(H1_HALO, H1_IN, H1_LEFT, H1_RIGHT)
    if_past(lambda: toward(ROWS, *send(row(H1P), halo_of(H1P))))
    toward(ROWS, *receive(row(H1), row(H0), halo_of(H1), halo_of(H0)))
    own_frames(H1, H0, w2, acc, ALL)
    arrived(H0_HALO, H0_TOP, H0_LOW)
    if_past(lambda: toward(ROWS, *send(row(H0P), halo_of(H0P))))
    if_past(lambda: toward(ROWS, *receive(row(H1P), halo_of(H1P))))
    result(1, past_later(H1P, w2, acc, ALL))
    pl.when(has_next)(lambda: [forward(p).wait_send() for p in range(15)] and None)
    toward(ROWS + SIDES, *sent(own))
    toward(ROWS, *sent(row(H0), halo_of(H0), row(H1), halo_of(H1)))

    @pl.when(has_prev)
    def _():
        toward(SIDES, *sent(past_pack))
        toward(ROWS, *sent(row(F1P), row(F0P), row(H1P), halo_of(H1P)))

    arrived(H0_MID)
    if_past(lambda: toward(ROWS, *receive(row(H0P), halo_of(H0P))))
    result(0, past_earlier(H0P, w2, acc, ALL))
    if_past(lambda: toward(ROWS, *sent(row(H0P), halo_of(H0P))))


def solution(mesh):
    groups, tiles_lon, tiles_lat = mesh.shape["tm"], mesh.shape["lon"], mesh.shape["lat"]

    def local(features, conv_first, conv_second):
        frames, rows, cols, chan = features.shape
        frame = (8, rows + 2, cols, chan)
        outer = 2 * T * rows + 2 * rows

        def kernel(*refs):
            block(groups, tiles_lon, tiles_lat, *refs)

        return pl.pallas_call(
            kernel,
            out_shape=pltpu.VMEM(features.shape, BF16),
            in_specs=[pl.BlockSpec(memory_space=pltpu.HBM)] * 3,
            out_specs=pl.BlockSpec(memory_space=pltpu.VMEM),
            scratch_shapes=[
                pltpu.VMEM(frame, BF16),
                pltpu.VMEM(frame, BF16),
                pltpu.VMEM(frame, BF16),
                pltpu.VMEM((4, 2, 2 * rows, chan), BF16),
                pltpu.VMEM((4, 6, 2 * rows, chan), BF16),
                pltpu.VMEM((4, 3, 2 * rows, chan), BF16),
                pltpu.VMEM(conv_first.shape, BF16),
                pltpu.VMEM(conv_second.shape, BF16),
                pltpu.VMEM(((cols - 2 * T) * rows, 2 * chan), F32),
                pltpu.VMEM((outer, 2 * chan), F32),
                pltpu.VMEM((rows * cols, 2 * chan), F32),
                pltpu.SemaphoreType.DMA((15,)),
                pltpu.SemaphoreType.DMA((15,)),
                pltpu.SemaphoreType.DMA((40,)),
                pltpu.SemaphoreType.DMA((40,)),
                pltpu.SemaphoreType.DMA((4,)),
                pltpu.SemaphoreType.REGULAR((8,)),
            ],
            compiler_params=pltpu.CompilerParams(
                collective_id=0, has_side_effects=True, vmem_limit_bytes=32 * 2**20),
            cost_estimate=pl.CostEstimate(
                flops=4 * frames * rows * cols * 27 * chan * chan, bytes_accessed=3 * 2**20, transcendentals=2**17),
            name="conv_block",
        )(*(pltpu.with_memory_space_constraint(x, pltpu.HBM) for x in (features, conv_first, conv_second)))

    placed = P("tm", "lat", "lon", None)
    return jax.shard_map(local, mesh=mesh, in_specs=(placed, P(), P()), out_specs=placed, check_vma=False)
```

time: 74.3 us -> 24.4 us (0.33)
  the two profiles are of different devices: /device:TPU:249 before, /device:TPU:65 now
where the time goes in v2:
time: 24.4 us; the launch traced here: 24.3 us
  Pallas kernels  23.6 us (97%)
  local copies, waits for them, and re-layouts  0.71 us (3%)
    pallas_call x1, Pallas kernels, local(): pl.pallas_call(kernel, out_shape=pltpu.VMEM(features.shape, BF16), in_spe...  23.6 us
    unnamed x1, local copies, waits for them, and re-layouts  0.71 us

profile of v2, /device:TPU:65, one launch (start us, length us, event | category | flops | bytes accessed | tf_op | source)
XLA Modules:
  0.0 24.3 jit_solution(1125531941499089835)
XLA Ops:
  0.0 23.6 %conv_block.1 = bf16[2,8,64,128]{3,2,1,0:T(8,128)(2,1)S(1)} custom-call(bf16[2,8,64,128]{3,2,1,0:T(8,128)(2,1)} %refs_0_.1, bf16[3,3,3,128,128]{4,3,2,1,0:T(8,128)(2,1)} %refs_1_.1, bf16[3,3,3,128,128]{4,3,2,1,0:T(8,128)(2,1)} %refs_2_.1), custom_call_target="tpu_custom_call" | custom-call | flops 1811939328 | bytes 3145728 | tf_op jit(solution)/shard_map/conv_block/pallas_call | solution.py:392
  23.6 0.7 %copy.5 = bf16[2,8,64,128]{3,2,1,0:T(8,128)(2,1)} copy(bf16[2,8,64,128]{3,2,1,0:T(8,128)(2,1)S(1)} %conv_block.1) | data formatting | bytes 524288

commit v3 on v2

--- a/solution.py
+++ b/solution.py
@@ -33,7 +33,6 @@
     later_e, later_w = jnp.logical_not(earlier_e), jnp.logical_not(earlier_w)
     far_e, far_w = lax.rem(lon, ring) == ring - 1, lax.rem(lon, ring) == 0
     near_e, near_w = jnp.logical_not(far_e), jnp.logical_not(far_w)
-    far = jnp.logical_or(far_e, far_w)
     up, down = lax.rem(lat + tiles_lat - 1, tiles_lat), lax.rem(lat + 1, tiles_lat)
 
     def device(d):
@@ -68,10 +67,33 @@
     def _():
         pl.semaphore_signal(barrier, inc=1, device_id={"tm": tm - 1}, device_id_type=MESH)
 
-    toward((U, D, W), greet)
-    pl.when(near_e)(lambda: greet(E))
-    pl.when(later_e)(lambda: toward((UE, DE), greet))
-    pl.when(later_w)(lambda: toward((UW, DW), greet))
+    origin = jnp.logical_and(tm == 0, jnp.logical_and(lon == 0, lat == 0))
+    awake = jnp.logical_not(origin)
+    lon_of, lat_of = {0: lon, 1: east, -1: west}, {0: lat, 1: down, -1: up}
+
+    def to_origin(d):
+        x, y = STEP[d]
+        return jnp.logical_and(tm == 0, jnp.logical_and(lon_of[x] == 0, lat_of[y] == 0))
+
+    def either(a, b):
+        return True if a is True or b is True else jnp.logical_or(a, b)
+
+    def greets_me(d):
+        first = {U: True, D: True, E: either(near_e, earlier_e), W: near_w}.get(d, earlier_e if STEP[d][0] > 0 else earlier_w)
+        if d in (D, DE, DW):
+            return either(origin, first)
+        return jnp.logical_and(either(origin, first), jnp.logical_not(to_origin(d)))
+
+    def i_greet(d):
+        first = {U: True, D: True, E: near_e, W: True}.get(d, later_e if STEP[d][0] > 0 else later_w)
+        if d in (D, DE, DW):
+            return jnp.logical_and(awake, first)
+        return jnp.logical_and(awake, either(first, to_origin(d)))
+
+    def toward_if(cond, ds, *runs):
+        toward(ds, *[lambda d, run=run: pl.when(cond(d))(lambda: run(d)) for run in runs])
+
+    toward_if(i_greet, range(8), greet)
 
     loads = [
         pltpu.make_async_copy(f_ref.at[1], xc.at[F1, pl.ds(1, rows)], load.at[0]),
@@ -252,12 +274,15 @@
     def shift(s, cuts):
         (shift_in if cuts is IN else shift_out if cuts is OUT else shift_all)(s)
 
-    def own_frames(later, earlier, w, acc, cuts):
-        shift(later, cuts)
-        shift(earlier, cuts)
-        v = taps(earlier, w, (2, 1), cuts)
+    def own_later(s, w, acc, cuts):
+        shift(s, cuts)
+        acc[:, chan:] = taps(s, w, (2,), cuts)
+
+    def own_earlier(s, w, acc, cuts):
+        shift(s, cuts)
+        v = taps(s, w, (2, 1), cuts)
         acc[:, :chan] = v[:, :chan]
-        acc[:, chan:] = v[:, chan:] + taps(later, w, (2,), cuts)
+        acc[:, chan:] += v[:, chan:]
 
     def past_later(s, w, acc, cuts):
         shift(s, cuts)
@@ -290,10 +315,11 @@
         copy.wait()
         make_pack(s)
 
-    heights = has_up.astype(I32) + has_down.astype(I32)
-    pl.semaphore_wait(
-        barrier,
-        1 + has_next.astype(I32) + near_w.astype(I32) + heights * (1 + earlier_e.astype(I32) + earlier_w.astype(I32)))
+    def count(d):
+        there = (has_up, True, has_down)[STEP[d][1] + 1]
+        return (greets_me(d) if there is True else jnp.logical_and(there, greets_me(d))).astype(I32)
+
+    pl.semaphore_wait(barrier, has_next.astype(I32) + sum(count(d) for d in range(8)))
 
     send_on(PACKS, F1_TOP, F1_LOW, F1_MID, F0_TOP, F0_LOW, F0_MID)
 
@@ -303,79 +329,89 @@
     def told(d):
         pl.semaphore_wait(entered.at[d], 1)
 
-    pl.when(far_e)(lambda: tell(E))
-    pl.when(earlier_e)(lambda: toward((UE, DE), tell))
-    pl.when(earlier_w)(lambda: toward((UW, DW), tell))
-
-    def known(*runs, rows=()):
-        toward((E, *rows), *runs)
-        pl.when(near_w)(lambda: toward((W,), *runs))
-        pl.when(earlier_e)(lambda: toward((UE, DE), *runs))
-        pl.when(earlier_w)(lambda: toward((UW, DW), *runs))
+    toward_if(lambda d: jnp.logical_not(i_greet(d)), range(8), tell)
+
+    def known(ds, *runs):
+        toward(ds, lambda d: pl.when(greets_me(d))(lambda: [run(d) for run in runs] and None))
+
+    def late(d):
+        far = jnp.logical_and(lon == 0, STEP[d][0] < 0)
+        return far if d in (D, DE, DW) else jnp.logical_or(far, to_origin(d))
+
+    def soon(d):
+        return jnp.logical_not(jnp.logical_or(greets_me(d), late(d)))
+
+    def last(d):
+        return jnp.logical_and(jnp.logical_not(greets_me(d)), late(d))
 
     def send_past_pack(d):
         if_past(lambda: past_pack(d).start())
 
-    def after_word(ds):
-        toward(ds, told, *send(own), send_past_pack)
-
-    known(*send(own), rows=ROWS)
+    def after_word(cond):
+        def run(d):
+            told(d)
+            own(d).start()
+            if d in RIM:
+                send_past_pack(d)
+        toward(ROWS + SIDES, lambda d: pl.when(cond(d))(lambda: run(d)))
+
+    known(ROWS + SIDES, *send(own))
     arrived(PACKS)
-    if_past(lambda: known(*send(past_pack)))
+    if_past(lambda: known(SIDES, *send(past_pack)))
     arrived(F1_TOP, F1_LOW)
     if_past(lambda: toward(ROWS, *send(row(F1P))))
     loads[2].wait()
     toward(ROWS, *receive(own))
-    own_frames(F1, F0, w1, acc_in, IN)
-    pl.when(later_e)(lambda: after_word((UE, DE)))
-    pl.when(jnp.logical_and(later_w, near_w))(lambda: after_word((UW, DW)))
+    own_later(F1, w1, acc_in, IN)
+    own_earlier(F0, w1, acc_in, IN)
+    after_word(soon)
     arrived(F1_MID)
     if_past(lambda: toward(ROWS, *receive(row(F1P))))
     hidden_in(H1, past_later(F1P, w1, acc_in, IN))
     send_on(H1_IN)
     arrived(F0_TOP, F0_LOW)
     if_past(lambda: toward(ROWS, *send(row(F0P))))
-    pl.when(far_w)(lambda: after_word((W, UW, DW)))
-
-    def outer_later():
-        toward(SIDES, *receive(own))
-        own_frames(F1, F0, w1, acc_out, OUT)
-        if_past(lambda: toward(SIDES, *receive(past_pack)))
-        hidden_out(H1, past_later(F1P, w1, acc_out, OUT))
-        send_on(H1_HALO, H1_LEFT, H1_RIGHT)
-        toward(ROWS, *send(row(H1), halo_of(H1)))
-
-    pl.when(jnp.logical_not(far))(outer_later)
+    after_word(last)
+
+    toward(SIDES, *receive(own))
+    own_later(F1, w1, acc_out, OUT)
+    own_earlier(F0, w1, acc_out, OUT)
+    if_past(lambda: toward(SIDES, *receive(past_pack)))
+    hidden_out(H1, past_later(F1P, w1, acc_out, OUT))
+    send_on(H1_HALO, H1_LEFT, H1_RIGHT)
+    toward(ROWS, *send(row(H1), halo_of(H1)))
     arrived(F0_MID)
     if_past(lambda: toward(ROWS, *receive(row(F0P))))
     hidden_in(H0, past_earlier(F0P, w1, acc_in, IN))
-    pl.when(far)(outer_later)
     hidden_out(H0, past_earlier(F0P, w1, acc_out, OUT))
     send_on(H0_HALO, H0_TOP, H0_LOW, H0_MID)
     toward(ROWS, *send(row(H0), halo_of(H0)))
 
     loads[3].wait()
-    arrived(H1_HALO, H1_IN, H1_LEFT, H1_RIGHT)
-    if_past(lambda: toward(ROWS, *send(row(H1P), halo_of(H1P))))
-    toward(ROWS, *receive(row(H1), row(H0), halo_of(H1), halo_of(H0)))
-    own_frames(H1, H0, w2, acc, ALL)
-    arrived(H0_HALO, H0_TOP, H0_LOW)
-    if_past(lambda: toward(ROWS, *send(row(H0P), halo_of(H0P))))
-    if_past(lambda: toward(ROWS, *receive(row(H1P), halo_of(H1P))))
-    result(1, past_later(H1P, w2, acc, ALL))
-    pl.when(has_next)(lambda: [forward(p).wait_send() for p in range(15)] and None)
+    pl.when(has_next)(lambda: [forward(p).wait_send() for p in range(H1_HALO)] and None)
     toward(ROWS + SIDES, *sent(own))
-    toward(ROWS, *sent(row(H0), halo_of(H0), row(H1), halo_of(H1)))
 
     @pl.when(has_prev)
     def _():
         toward(SIDES, *sent(past_pack))
-        toward(ROWS, *sent(row(F1P), row(F0P), row(H1P), halo_of(H1P)))
-
+        toward(ROWS, *sent(row(F1P), row(F0P)))
+
+    toward(ROWS, *receive(row(H1), halo_of(H1)))
+    own_later(H1, w2, acc, ALL)
+    arrived(H1_HALO, H1_IN, H1_LEFT, H1_RIGHT)
+    if_past(lambda: toward(ROWS, *send(row(H1P), halo_of(H1P))))
+    arrived(H0_HALO, H0_TOP, H0_LOW)
+    if_past(lambda: toward(ROWS, *send(row(H0P), halo_of(H0P))))
+    toward(ROWS, *receive(row(H0), halo_of(H0)))
+    own_earlier(H0, w2, acc, ALL)
+    pl.when(has_next)(lambda: [forward(p).wait_send() for p in range(H1_HALO, 15)] and None)
+    toward(ROWS, *sent(row(H0), halo_of(H0), row(H1), halo_of(H1)))
+    if_past(lambda: toward(ROWS, *receive(row(H1P), halo_of(H1P))))
+    result(1, past_later(H1P, w2, acc, ALL))
     arrived(H0_MID)
     if_past(lambda: toward(ROWS, *receive(row(H0P), halo_of(H0P))))
     result(0, past_earlier(H0P, w2, acc, ALL))
-    if_past(lambda: toward(ROWS, *sent(row(H0P), halo_of(H0P))))
+    if_past(lambda: toward(ROWS, *sent(row(H1P), halo_of(H1P), row(H0P), halo_of(H0P))))
 
 
 def solution(mesh):

time: 24.4 us -> 23.6 us (0.967)
  the two profiles are of different devices: /device:TPU:65 before, /device:TPU:321 now
where the time goes in v3:
time: 23.6 us; the launch traced here: 23.4 us
  Pallas kernels  22.7 us (96%)
  local copies, waits for them, and re-layouts  0.71 us (3%)
    pallas_call x1, Pallas kernels, local(): pl.pallas_call(kernel, out_shape=pltpu.VMEM(features.shape, BF16), in_spe...  22.7 us
    unnamed x1, local copies, waits for them, and re-layouts  0.71 us

profile of v3, /device:TPU:321, one launch (start us, length us, event | category | flops | bytes accessed | tf_op | source)
XLA Modules:
  0.0 23.4 jit_solution(2880382056752423025)
XLA Ops:
  0.0 22.7 %conv_block.1 = bf16[2,8,64,128]{3,2,1,0:T(8,128)(2,1)S(1)} custom-call(bf16[2,8,64,128]{3,2,1,0:T(8,128)(2,1)} %refs_0_.1, bf16[3,3,3,128,128]{4,3,2,1,0:T(8,128)(2,1)} %refs_1_.1, bf16[3,3,3,128,128]{4,3,2,1,0:T(8,128)(2,1)} %refs_2_.1), custom_call_target="tpu_custom_call" | custom-call | flops 1811939328 | bytes 3145728 | tf_op jit(solution)/shard_map/conv_block/pallas_call | solution.py:428
  22.7 0.7 %copy.5 = bf16[2,8,64,128]{3,2,1,0:T(8,128)(2,1)} copy(bf16[2,8,64,128]{3,2,1,0:T(8,128)(2,1)S(1)} %conv_block.1) | data formatting | bytes 524288

commit v4 on v3

--- a/solution.py
+++ b/solution.py
@@ -95,6 +95,15 @@
 
     toward_if(i_greet, range(8), greet)
 
+    EAST, WEST = (E, UE, DE), (W, UW, DW)
+    from_last, to_first = jnp.logical_and(lon == 0, has_prev), jnp.logical_and(lon == tiles_lon - 1, has_next)
+
+    @pl.when(from_last)
+    def _():
+        toward(WEST, lambda d: pl.semaphore_signal(
+            barrier, inc=1, device_id={"tm": tm - 1, **device(d)}, device_id_type=MESH))
+
+
     loads = [
         pltpu.make_async_copy(f_ref.at[1], xc.at[F1, pl.ds(1, rows)], load.at[0]),
         pltpu.make_async_copy(f_ref.at[0], xc.at[F0, pl.ds(1, rows)], load.at[1]),
@@ -108,11 +117,11 @@
         return pltpu.make_async_remote_copy(
             src_ref=src, dst_ref=dst, send_sem=sems[0].at[i], recv_sem=sems[1].at[i], device_id=to, device_id_type=MESH)
 
-    body, both, past = pl.ds(1, rows), pl.ds(F0, 2), pl.ds(F0P, 2)
+    both, past = pl.ds(F0, 2), pl.ds(F0P, 2)
     left, inner, right = pl.ds(0, T), pl.ds(T, cols - 2 * T), pl.ds(cols - T, T)
 
     PACKS, F1_TOP, F1_LOW, F1_MID, F0_TOP, F0_LOW, F0_MID = range(7)
-    H1_HALO, H1_IN, H1_LEFT, H1_RIGHT, H0_HALO, H0_TOP, H0_LOW, H0_MID = range(7, 15)
+    H1_HALO, H1_IN, H1_TOP, H1_LOW, H1_LEFT, H1_RIGHT, H0_HALO, H0_TOP, H0_LOW, H0_MID = range(7, 17)
 
     def forward(i):
         def at(s, *where):
@@ -124,7 +133,8 @@
             F1_TOP: lambda: at(F1, 1), F1_LOW: lambda: at(F1, rows), F1_MID: lambda: at(F1, mid),
             F0_TOP: lambda: at(F0, 1), F0_LOW: lambda: at(F0, rows), F0_MID: lambda: at(F0, mid),
             H1_HALO: lambda: (halo.at[H1 - 4, 0], halo.at[H1P - 4, 0]),
-            H1_IN: lambda: at(H1, body, inner), H1_LEFT: lambda: at(H1, body, left), H1_RIGHT: lambda: at(H1, body, right),
+            H1_IN: lambda: at(H1, mid, inner), H1_TOP: lambda: at(H1, 1), H1_LOW: lambda: at(H1, rows),
+            H1_LEFT: lambda: at(H1, mid, left), H1_RIGHT: lambda: at(H1, mid, right),
             H0_HALO: lambda: (halo.at[H0 - 4, 0], halo.at[H0P - 4, 0]),
             H0_TOP: lambda: at(H0, 1), H0_LOW: lambda: at(H0, rows), H0_MID: lambda: at(H0, mid),
         }[i]()
@@ -145,6 +155,10 @@
 
     def past_pack(d):
         return remote(pack.at[past, int(STEP[d][0] > 0)], rim.at[past, RIM[d]], (lsend, lrecv), 8 + d, device(d))
+
+    def direct_pack(d):
+        return remote(
+            pack.at[both, 1], rim.at[past, RIM[d]], (lsend, lrecv), 8 + d, {"tm": lax.rem(tm + 1, groups), **device(d)})
 
     def row(s):
         base = {F1P: 8, F0P: 16}.get(s, 24 + 4 * (s - 4))
@@ -220,7 +234,7 @@
         return halo[s - 4, 0, r - 1:r], halo[s - 4, 0, rows + r - 1:rows + r]
 
     def shift_in(s):
-        for r in range(rows + 2):
+        for r in range(1, rows + 1):
             x = xc[s, r]
             xl[s, r, T:cols - T] = x[T - 1:cols - T - 1]
             xr[s, r, T:cols - T] = x[T + 1:cols - T + 1]
@@ -229,6 +243,9 @@
         for r in range(rows + 2):
             before, after = beside(s, r)
             x = xc[s, r]
+            if r in (0, rows + 1):
+                xl[s, r, T:cols - T] = x[T - 1:cols - T - 1]
+                xr[s, r, T:cols - T] = x[T + 1:cols - T + 1]
             xl[s, r, 0:T] = jnp.concatenate([before, x[:T - 1]], axis=0)
             xl[s, r, cols - T:] = x[cols - T - 1:cols - 1]
             xr[s, r, 0:T] = x[1:T + 1]
@@ -257,12 +274,14 @@
         return jnp.concatenate(
             [jnp.concatenate([wests[c][b], easts[c][b]], axis=0).astype(BF16) for b in range(3) for c in range(3)], axis=1)
 
-    IN, OUT, ALL = (slice(T, cols - T),), (slice(0, T), slice(cols - T, cols)), (slice(0, cols),)
+    MID, INNER = slice(1, rows - 1), slice(T, cols - T)
+    IN = ((MID, INNER),)
+    OUT = ((slice(0, rows), slice(0, T)), (slice(0, rows), slice(cols - T, cols)), (slice(0, 1), INNER), (slice(rows - 1, rows), INNER))
+    ALL = ((slice(0, rows), slice(0, cols)),)
 
     def taken(ref, s, b, cuts):
-        some = [ref[s, b:b + rows, c] for c in cuts]
-        some = some[0] if len(some) == 1 else jnp.concatenate(some, axis=1)
-        return some.reshape(-1, chan)
+        some = [ref[s, r.start + b:r.stop + b, c].reshape(-1, chan) for r, c in cuts]
+        return some[0] if len(some) == 1 else jnp.concatenate(some, axis=0)
 
     def taps(s, w, times, cuts):
         x = jnp.concatenate([taken(ref, s, b, cuts) for b in range(3) for ref in (xl, xc, xr)], axis=1)
@@ -297,15 +316,21 @@
     def silu(v):
         return (v / (1 + jnp.exp(-v))).astype(BF16)
 
+    def hidden_part(s, h, cuts):
+        at = 0
+        for r, c in cuts:
+            high, wide = r.stop - r.start, c.stop - c.start
+            xc[s, r.start + 1:r.stop + 1, c] = h[at:at + high * wide].reshape(high, wide, chan)
+            at += high * wide
+        return at
+
     def hidden_in(s, v):
-        xc[s, 1:rows + 1, T:cols - T] = silu(v).reshape(rows, cols - 2 * T, chan)
+        hidden_part(s, silu(v), IN)
 
     def hidden_out(s, v):
         h = silu(v)
-        halo[s - 4, 0] = h[2 * T * rows:]
-        h = h[:2 * T * rows].reshape(rows, 2 * T, chan)
-        xc[s, 1:rows + 1, 0:T] = h[:, :T]
-        xc[s, 1:rows + 1, cols - T:] = h[:, T:]
+        at = hidden_part(s, h, OUT)
+        halo[s - 4, 0] = h[at:]
 
     def result(t, v):
         x = xc[(F0, F1)[t], 1:rows + 1].reshape(-1, chan).astype(F32) + v
@@ -319,9 +344,13 @@
         there = (has_up, True, has_down)[STEP[d][1] + 1]
         return (greets_me(d) if there is True else jnp.logical_and(there, greets_me(d))).astype(I32)
 
-    pl.semaphore_wait(barrier, has_next.astype(I32) + sum(count(d) for d in range(8)))
-
-    send_on(PACKS, F1_TOP, F1_LOW, F1_MID, F0_TOP, F0_LOW, F0_MID)
+    pl.semaphore_wait(
+        barrier, has_next.astype(I32) + sum(count(d) for d in range(8))
+        + to_first.astype(I32) * (1 + has_up.astype(I32) + has_down.astype(I32)))
+
+    send_on(PACKS)
+    pl.when(to_first)(lambda: toward(EAST, *send(direct_pack)))
+    send_on(F1_TOP, F1_LOW, F1_MID, F0_TOP, F0_LOW, F0_MID)
 
     def tell(d):
         pl.semaphore_signal(entered.at[BACK[d]], inc=1, device_id=device(d), device_id_type=MESH)
@@ -345,7 +374,10 @@
         return jnp.logical_and(jnp.logical_not(greets_me(d)), late(d))
 
     def send_past_pack(d):
-        if_past(lambda: past_pack(d).start())
+        if d in EAST:
+            pl.when(jnp.logical_and(has_prev, inland))(lambda: past_pack(d).start())
+        else:
+            if_past(lambda: past_pack(d).start())
 
     def after_word(cond):
         def run(d):
@@ -356,33 +388,40 @@
         toward(ROWS + SIDES, lambda d: pl.when(cond(d))(lambda: run(d)))
 
     known(ROWS + SIDES, *send(own))
+    loads[2].wait()
+    own_later(F1, w1, acc_in, IN)
+    own_earlier(F0, w1, acc_in, IN)
     arrived(PACKS)
-    if_past(lambda: known(SIDES, *send(past_pack)))
+    if_past(lambda: known(WEST, *send(past_pack)))
+    inland = lon < tiles_lon - 1
+    pl.when(jnp.logical_and(has_prev, inland))(lambda: known(EAST, *send(past_pack)))
     arrived(F1_TOP, F1_LOW)
     if_past(lambda: toward(ROWS, *send(row(F1P))))
-    loads[2].wait()
-    toward(ROWS, *receive(own))
-    own_later(F1, w1, acc_in, IN)
-    own_earlier(F0, w1, acc_in, IN)
     after_word(soon)
     arrived(F1_MID)
-    if_past(lambda: toward(ROWS, *receive(row(F1P))))
     hidden_in(H1, past_later(F1P, w1, acc_in, IN))
     send_on(H1_IN)
     arrived(F0_TOP, F0_LOW)
     if_past(lambda: toward(ROWS, *send(row(F0P))))
     after_word(last)
 
-    toward(SIDES, *receive(own))
+    toward(ROWS + SIDES, *receive(own))
     own_later(F1, w1, acc_out, OUT)
     own_earlier(F0, w1, acc_out, OUT)
+
+    def inner_earlier():
+        arrived(F0_MID)
+        hidden_in(H0, past_earlier(F0P, w1, acc_in, IN))
+
+    far = jnp.logical_or(far_e, far_w)
+    pl.when(far)(inner_earlier)
     if_past(lambda: toward(SIDES, *receive(past_pack)))
+    if_past(lambda: toward(ROWS, *receive(row(F1P))))
     hidden_out(H1, past_later(F1P, w1, acc_out, OUT))
-    send_on(H1_HALO, H1_LEFT, H1_RIGHT)
+    send_on(H1_HALO, H1_TOP, H1_LOW, H1_LEFT, H1_RIGHT)
     toward(ROWS, *send(row(H1), halo_of(H1)))
-    arrived(F0_MID)
+    pl.when(jnp.logical_not(far))(inner_earlier)
     if_past(lambda: toward(ROWS, *receive(row(F0P))))
-    hidden_in(H0, past_earlier(F0P, w1, acc_in, IN))
     hidden_out(H0, past_earlier(F0P, w1, acc_out, OUT))
     send_on(H0_HALO, H0_TOP, H0_LOW, H0_MID)
     toward(ROWS, *send(row(H0), halo_of(H0)))
@@ -390,23 +429,26 @@
     loads[3].wait()
     pl.when(has_next)(lambda: [forward(p).wait_send() for p in range(H1_HALO)] and None)
     toward(ROWS + SIDES, *sent(own))
+    pl.when(to_first)(lambda: toward(EAST, *sent(direct_pack)))
 
     @pl.when(has_prev)
     def _():
-        toward(SIDES, *sent(past_pack))
+        toward(WEST, *sent(past_pack))
+        pl.when(inland)(lambda: toward(EAST, *sent(past_pack)))
         toward(ROWS, *sent(row(F1P), row(F0P)))
 
+    arrived(H1_HALO, H1_TOP, H1_LOW)
+    if_past(lambda: toward(ROWS, *send(row(H1P), halo_of(H1P))))
     toward(ROWS, *receive(row(H1), halo_of(H1)))
     own_later(H1, w2, acc, ALL)
-    arrived(H1_HALO, H1_IN, H1_LEFT, H1_RIGHT)
-    if_past(lambda: toward(ROWS, *send(row(H1P), halo_of(H1P))))
     arrived(H0_HALO, H0_TOP, H0_LOW)
     if_past(lambda: toward(ROWS, *send(row(H0P), halo_of(H0P))))
     toward(ROWS, *receive(row(H0), halo_of(H0)))
     own_earlier(H0, w2, acc, ALL)
-    pl.when(has_next)(lambda: [forward(p).wait_send() for p in range(H1_HALO, 15)] and None)
+    pl.when(has_next)(lambda: [forward(p).wait_send() for p in range(H1_HALO, 17)] and None)
     toward(ROWS, *sent(row(H0), halo_of(H0), row(H1), halo_of(H1)))
     if_past(lambda: toward(ROWS, *receive(row(H1P), halo_of(H1P))))
+    arrived(H1_IN, H1_LEFT, H1_RIGHT)
     result(1, past_later(H1P, w2, acc, ALL))
     arrived(H0_MID)
     if_past(lambda: toward(ROWS, *receive(row(H0P), halo_of(H0P))))
@@ -420,7 +462,8 @@
     def local(features, conv_first, conv_second):
         frames, rows, cols, chan = features.shape
         frame = (8, rows + 2, cols, chan)
-        outer = 2 * T * rows + 2 * rows
+        inner = (cols - 2 * T) * (rows - 2)
+        outer = rows * cols - inner + 2 * rows
 
         def kernel(*refs):
             block(groups, tiles_lon, tiles_lat, *refs)
@@ -439,11 +482,11 @@
                 pltpu.VMEM((4, 3, 2 * rows, chan), BF16),
                 pltpu.VMEM(conv_first.shape, BF16),
                 pltpu.VMEM(conv_second.shape, BF16),
-                pltpu.VMEM(((cols - 2 * T) * rows, 2 * chan), F32),
+                pltpu.VMEM((inner, 2 * chan), F32),
                 pltpu.VMEM((outer, 2 * chan), F32),
                 pltpu.VMEM((rows * cols, 2 * chan), F32),
-                pltpu.SemaphoreType.DMA((15,)),
-                pltpu.SemaphoreType.DMA((15,)),
+                pltpu.SemaphoreType.DMA((17,)),
+                pltpu.SemaphoreType.DMA((17,)),
                 pltpu.SemaphoreType.DMA((40,)),
                 pltpu.SemaphoreType.DMA((40,)),
                 pltpu.SemaphoreType.DMA((4,)),

time: 23.6 us -> 23.3 us (0.987)
  the two profiles are of different devices: /device:TPU:321 before, /device:TPU:381 now
where the time goes in v4:
time: 23.3 us; the launch traced here: 23.1 us
  Pallas kernels  22.4 us (96%)
  local copies, waits for them, and re-layouts  0.71 us (3%)
    pallas_call x1, Pallas kernels, local(): pl.pallas_call(kernel, out_shape=pltpu.VMEM(features.shape, BF16), in_spe...  22.4 us
    unnamed x1, local copies, waits for them, and re-layouts  0.71 us

profile of v4, /device:TPU:381, one launch (start us, length us, event | category | flops | bytes accessed | tf_op | source)
XLA Modules:
  0.0 23.1 jit_solution(18261874830523057604)
XLA Ops:
  0.0 22.4 %conv_block.1 = bf16[2,8,64,128]{3,2,1,0:T(8,128)(2,1)S(1)} custom-call(bf16[2,8,64,128]{3,2,1,0:T(8,128)(2,1)} %refs_0_.1, bf16[3,3,3,128,128]{4,3,2,1,0:T(8,128)(2,1)} %refs_1_.1, bf16[3,3,3,128,128]{4,3,2,1,0:T(8,128)(2,1)} %refs_2_.1), custom_call_target="tpu_custom_call" | custom-call | flops 1811939328 | bytes 3145728 | tf_op jit(solution)/shard_map/conv_block/pallas_call | solution.py:471
  22.4 0.7 %copy.5 = bf16[2,8,64,128]{3,2,1,0:T(8,128)(2,1)} copy(bf16[2,8,64,128]{3,2,1,0:T(8,128)(2,1)S(1)} %conv_block.1) | data formatting | bytes 524288

commit v5 on v4

--- a/solution.py
+++ b/solution.py
@@ -95,6 +95,20 @@
 
     toward_if(i_greet, range(8), greet)
 
+    opposite, across, relay = (lax.rem(lon + k, tiles_lon) for k in (ring, ring + 1, ring - 1))
+
+    def relays(d):
+        return jnp.logical_not(jnp.logical_and(tm == 0, jnp.logical_and(across == 0, lat_of[STEP[d][1]] == 0)))
+
+    @pl.when(far_e)
+    def _():
+        pl.semaphore_signal(barrier, inc=1, device_id={"lon": opposite}, device_id_type=MESH)
+
+    @pl.when(jnp.logical_and(far_w, awake))
+    def _():
+        toward((W, UW, DW), lambda d: pl.semaphore_signal(
+            barrier, inc=1, device_id={**device(d), "lon": relay}, device_id_type=MESH))
+
     EAST, WEST = (E, UE, DE), (W, UW, DW)
     from_last, to_first = jnp.logical_and(lon == 0, has_prev), jnp.logical_and(lon == tiles_lon - 1, has_next)
 
@@ -103,6 +117,13 @@
         toward(WEST, lambda d: pl.semaphore_signal(
             barrier, inc=1, device_id={"tm": tm - 1, **device(d)}, device_id_type=MESH))
 
+
+    over = tiles_lat // 2
+    from_over, to_over = jnp.logical_and(lat == over - 1, has_prev), jnp.logical_and(lat == over, has_next)
+
+    @pl.when(from_over)
+    def _():
+        pl.semaphore_signal(barrier, inc=1, device_id={"tm": tm - 1, "lat": down}, device_id_type=MESH)
 
     loads = [
         pltpu.make_async_copy(f_ref.at[1], xc.at[F1, pl.ds(1, rows)], load.at[0]),
@@ -176,6 +197,23 @@
                 (lsend, lrecv), 26 + 4 * (s - 4) + int(d == D), device(d))
         return make
 
+    def straight(s):
+        to, base = {"tm": lax.rem(tm + 1, groups), "lat": up}, {F1: 10, F0: 18}.get(s, 24 + 4 * (NEXT[s] - 4))
+        copies = [remote(xc.at[s, 1], xc.at[NEXT[s], rows + 1], (lsend, lrecv), base, to)]
+        if s > H1P:
+            copies.append(remote(halo.at[s - 4, 0], halo.at[NEXT[s] - 4, 2], (lsend, lrecv), base + 2, to))
+        return copies
+
+    def go_straight(s):
+        pl.when(to_over)(lambda: [copy.start() for copy in straight(s)] and None)
+
+    def gone_straight(*ss):
+        pl.when(to_over)(lambda: [copy.wait_send() for s in ss for copy in straight(s)] and None)
+
+    def pass_on(*runs):
+        toward((D,), *runs)
+        pl.when(lat != over)(lambda: toward((U,), *runs))
+
     def send(*makes):
         return [lambda d, make=make: make(d).start() for make in makes]
 
@@ -346,26 +384,38 @@
 
     pl.semaphore_wait(
         barrier, has_next.astype(I32) + sum(count(d) for d in range(8))
-        + to_first.astype(I32) * (1 + has_up.astype(I32) + has_down.astype(I32)))
+        + far_e.astype(I32) * (1 + relays(E).astype(I32) + jnp.logical_and(has_up, relays(UE)).astype(I32)
+                               + jnp.logical_and(has_down, relays(DE)).astype(I32))
+        + to_over.astype(I32) + to_first.astype(I32) * (1 + has_up.astype(I32) + has_down.astype(I32)))
 
     send_on(PACKS)
     pl.when(to_first)(lambda: toward(EAST, *send(direct_pack)))
-    send_on(F1_TOP, F1_LOW, F1_MID, F0_TOP, F0_LOW, F0_MID)
+    send_on(F1_TOP, F1_LOW)
+    go_straight(F1)
+    send_on(F1_MID, F0_TOP, F0_LOW)
+    go_straight(F0)
+    send_on(F0_MID)
 
     def tell(d):
-        pl.semaphore_signal(entered.at[BACK[d]], inc=1, device_id=device(d), device_id_type=MESH)
+        to = device(d)
+        if d in EAST:
+            to["lon"] = jnp.where(far_e, across, east)
+        pl.semaphore_signal(entered.at[BACK[d]], inc=1, device_id=to, device_id_type=MESH)
+
+    def i_tell(d):
+        quiet = jnp.logical_not(i_greet(d))
+        return jnp.where(far_e, relays(d), quiet) if d in EAST else quiet
 
     def told(d):
         pl.semaphore_wait(entered.at[d], 1)
 
-    toward_if(lambda d: jnp.logical_not(i_greet(d)), range(8), tell)
+    toward_if(i_tell, range(8), tell)
 
     def known(ds, *runs):
         toward(ds, lambda d: pl.when(greets_me(d))(lambda: [run(d) for run in runs] and None))
 
     def late(d):
-        far = jnp.logical_and(lon == 0, STEP[d][0] < 0)
-        return far if d in (D, DE, DW) else jnp.logical_or(far, to_origin(d))
+        return False if d in (D, DE, DW) else to_origin(d)
 
     def soon(d):
         return jnp.logical_not(jnp.logical_or(greets_me(d), late(d)))
@@ -396,13 +446,13 @@
     inland = lon < tiles_lon - 1
     pl.when(jnp.logical_and(has_prev, inland))(lambda: known(EAST, *send(past_pack)))
     arrived(F1_TOP, F1_LOW)
-    if_past(lambda: toward(ROWS, *send(row(F1P))))
+    if_past(lambda: pass_on(*send(row(F1P))))
     after_word(soon)
     arrived(F1_MID)
     hidden_in(H1, past_later(F1P, w1, acc_in, IN))
     send_on(H1_IN)
     arrived(F0_TOP, F0_LOW)
-    if_past(lambda: toward(ROWS, *send(row(F0P))))
+    if_past(lambda: pass_on(*send(row(F0P))))
     after_word(last)
 
     toward(ROWS + SIDES, *receive(own))
@@ -418,34 +468,40 @@
     if_past(lambda: toward(SIDES, *receive(past_pack)))
     if_past(lambda: toward(ROWS, *receive(row(F1P))))
     hidden_out(H1, past_later(F1P, w1, acc_out, OUT))
-    send_on(H1_HALO, H1_TOP, H1_LOW, H1_LEFT, H1_RIGHT)
+    send_on(H1_HALO, H1_TOP, H1_LOW)
+    go_straight(H1)
+    send_on(H1_LEFT, H1_RIGHT)
     toward(ROWS, *send(row(H1), halo_of(H1)))
     pl.when(jnp.logical_not(far))(inner_earlier)
     if_past(lambda: toward(ROWS, *receive(row(F0P))))
     hidden_out(H0, past_earlier(F0P, w1, acc_out, OUT))
-    send_on(H0_HALO, H0_TOP, H0_LOW, H0_MID)
+    send_on(H0_HALO, H0_TOP, H0_LOW)
+    go_straight(H0)
+    send_on(H0_MID)
     toward(ROWS, *send(row(H0), halo_of(H0)))
 
     loads[3].wait()
     pl.when(has_next)(lambda: [forward(p).wait_send() for p in range(H1_HALO)] and None)
     toward(ROWS + SIDES, *sent(own))
     pl.when(to_first)(lambda: toward(EAST, *sent(direct_pack)))
+    gone_straight(F1, F0)
 
     @pl.when(has_prev)
     def _():
         toward(WEST, *sent(past_pack))
         pl.when(inland)(lambda: toward(EAST, *sent(past_pack)))
-        toward(ROWS, *sent(row(F1P), row(F0P)))
+        pass_on(*sent(row(F1P), row(F0P)))
 
     arrived(H1_HALO, H1_TOP, H1_LOW)
-    if_past(lambda: toward(ROWS, *send(row(H1P), halo_of(H1P))))
+    if_past(lambda: pass_on(*send(row(H1P), halo_of(H1P))))
     toward(ROWS, *receive(row(H1), halo_of(H1)))
     own_later(H1, w2, acc, ALL)
     arrived(H0_HALO, H0_TOP, H0_LOW)
-    if_past(lambda: toward(ROWS, *send(row(H0P), halo_of(H0P))))
+    if_past(lambda: pass_on(*send(row(H0P), halo_of(H0P))))
     toward(ROWS, *receive(row(H0), halo_of(H0)))
     own_earlier(H0, w2, acc, ALL)
     pl.when(has_next)(lambda: [forward(p).wait_send() for p in range(H1_HALO, 17)] and None)
+    gone_straight(H1, H0)
     toward(ROWS, *sent(row(H0), halo_of(H0), row(H1), halo_of(H1)))
     if_past(lambda: toward(ROWS, *receive(row(H1P), halo_of(H1P))))
     arrived(H1_IN, H1_LEFT, H1_RIGHT)
@@ -453,7 +509,7 @@
     arrived(H0_MID)
     if_past(lambda: toward(ROWS, *receive(row(H0P), halo_of(H0P))))
     result(0, past_earlier(H0P, w2, acc, ALL))
-    if_past(lambda: toward(ROWS, *sent(row(H1P), halo_of(H1P), row(H0P), halo_of(H0P))))
+    if_past(lambda: pass_on(*sent(row(H1P), halo_of(H1P), row(H0P), halo_of(H0P))))
 
 
 def solution(mesh):

time: 23.3 us -> 23.3 us (level)
  the two profiles are of different devices: /device:TPU:381 before, /device:TPU:1 now
where the time goes in v5:
time: 23.3 us; the launch traced here: 23.2 us
  Pallas kernels  22.5 us (97%)
  local copies, waits for them, and re-layouts  0.71 us (3%)
    pallas_call x1, Pallas kernels, local(): pl.pallas_call(kernel, out_shape=pltpu.VMEM(features.shape, BF16), in_spe...  22.5 us
    unnamed x1, local copies, waits for them, and re-layouts  0.71 us

profile of v5, /device:TPU:1, one launch (start us, length us, event | category | flops | bytes accessed | tf_op | source)
XLA Modules:
  0.0 23.2 jit_solution(14842436549058449382)
XLA Ops:
  0.0 22.5 %conv_block.1 = bf16[2,8,64,128]{3,2,1,0:T(8,128)(2,1)S(1)} custom-call(bf16[2,8,64,128]{3,2,1,0:T(8,128)(2,1)} %refs_0_.1, bf16[3,3,3,128,128]{4,3,2,1,0:T(8,128)(2,1)} %refs_1_.1, bf16[3,3,3,128,128]{4,3,2,1,0:T(8,128)(2,1)} %refs_2_.1), custom_call_target="tpu_custom_call" | custom-call | flops 1811939328 | bytes 3145728 | tf_op jit(solution)/shard_map/conv_block/pallas_call | solution.py:527
  22.5 0.7 %copy.5 = bf16[2,8,64,128]{3,2,1,0:T(8,128)(2,1)} copy(bf16[2,8,64,128]{3,2,1,0:T(8,128)(2,1)S(1)} %conv_block.1) | data formatting | bytes 524288

commit v6 on v5

--- a/solution.py
+++ b/solution.py
@@ -404,7 +404,23 @@
 
     def i_tell(d):
         quiet = jnp.logical_not(i_greet(d))
-        return jnp.where(far_e, relays(d), quiet) if d in EAST else quiet
+        if d in EAST:
+            return jnp.where(far_e, relays(d), quiet)
+        return jnp.logical_and(quiet, awake) if d in WEST else quiet
+
+    helper = jnp.logical_and(tm == 0, jnp.logical_and(lon == 0, lat == 1))
+
+    def direct(d):
+        if d not in (E, UE):
+            return True
+        return jnp.logical_not(jnp.logical_and(to_origin(d), lon == tiles_lon - 1))
+
+    def helped():
+        return [
+            pltpu.make_async_remote_copy(
+                src_ref=rim.at[both, src], dst_ref=rim.at[both, dst], send_sem=lsend.at[40 + i], recv_sem=lrecv.at[d],
+                device_id={"lat": up}, device_id_type=MESH)
+            for i, (src, dst, d) in enumerate(((RIM[DE], RIM[E], E), (RIM[E], RIM[UE], UE)))]
 
     def told(d):
         pl.semaphore_wait(entered.at[d], 1)
@@ -421,7 +437,8 @@
         return jnp.logical_not(jnp.logical_or(greets_me(d), late(d)))
 
     def last(d):
-        return jnp.logical_and(jnp.logical_not(greets_me(d)), late(d))
+        slow = jnp.logical_and(jnp.logical_not(greets_me(d)), late(d))
+        return slow if direct(d) is True else jnp.logical_and(slow, direct(d))
 
     def send_past_pack(d):
         if d in EAST:
@@ -456,6 +473,7 @@
     after_word(last)
 
     toward(ROWS + SIDES, *receive(own))
+    pl.when(helper)(lambda: [copy.start() for copy in helped()] and None)
     own_later(F1, w1, acc_out, OUT)
     own_earlier(F0, w1, acc_out, OUT)
 
@@ -482,7 +500,9 @@
 
     loads[3].wait()
     pl.when(has_next)(lambda: [forward(p).wait_send() for p in range(H1_HALO)] and None)
-    toward(ROWS + SIDES, *sent(own))
+    toward((U, D, DE, W, UW, DW), *sent(own))
+    toward_if(direct, (E, UE), *sent(own))
+    pl.when(helper)(lambda: [copy.wait_send() for copy in helped()] and None)
     pl.when(to_first)(lambda: toward(EAST, *sent(direct_pack)))
     gone_straight(F1, F0)
 
@@ -543,7 +563,7 @@
                 pltpu.VMEM((rows * cols, 2 * chan), F32),
                 pltpu.SemaphoreType.DMA((17,)),
                 pltpu.SemaphoreType.DMA((17,)),
-                pltpu.SemaphoreType.DMA((40,)),
+                pltpu.SemaphoreType.DMA((42,)),
                 pltpu.SemaphoreType.DMA((40,)),
                 pltpu.SemaphoreType.DMA((4,)),
                 pltpu.SemaphoreType.REGULAR((8,)),

time: 23.3 us -> 22.2 us (0.953)
  the two profiles are of different devices: /device:TPU:1 before, /device:TPU:192 now
where the time goes in v6:
time: 22.2 us; the launch traced here: 22.1 us
  Pallas kernels  21.4 us (96%)
  local copies, waits for them, and re-layouts  0.71 us (3%)
    pallas_call x1, Pallas kernels, local(): pl.pallas_call(kernel, out_shape=pltpu.VMEM(features.shape, BF16), in_spe...  21.4 us
    unnamed x1, local copies, waits for them, and re-layouts  0.71 us

profile of v6, /device:TPU:192, one launch (start us, length us, event | category | flops | bytes accessed | tf_op | source)
XLA Modules:
  0.0 22.1 jit_solution(9271526251823957921)
XLA Ops:
  0.0 21.4 %conv_block.1 = bf16[2,8,64,128]{3,2,1,0:T(8,128)(2,1)S(1)} custom-call(bf16[2,8,64,128]{3,2,1,0:T(8,128)(2,1)} %refs_0_.1, bf16[3,3,3,128,128]{4,3,2,1,0:T(8,128)(2,1)} %refs_1_.1, bf16[3,3,3,128,128]{4,3,2,1,0:T(8,128)(2,1)} %refs_2_.1), custom_call_target="tpu_custom_call" | custom-call | flops 1811939328 | bytes 3145728 | tf_op jit(solution)/shard_map/conv_block/pallas_call | solution.py:547
  21.4 0.7 %copy.5 = bf16[2,8,64,128]{3,2,1,0:T(8,128)(2,1)} copy(bf16[2,8,64,128]{3,2,1,0:T(8,128)(2,1)S(1)} %conv_block.1) | data formatting | bytes 524288

commit v7 on v6

--- a/solution.py
+++ b/solution.py
@@ -352,7 +352,8 @@
         return acc[:, :chan] + taps(s, w, (0,), cuts)
 
     def silu(v):
-        return (v / (1 + jnp.exp(-v))).astype(BF16)
+        half = 0.5 * v
+        return (half + half * jnp.tanh(half)).astype(BF16)
 
     def hidden_part(s, h, cuts):
         at = 0

time: 22.2 us -> 22.2 us (level)
  no operation moved by 1% of the time
where the time goes in v7:
time: 22.2 us; the launch traced here: 22.1 us
  Pallas kernels  21.3 us (96%)
  local copies, waits for them, and re-layouts  0.71 us (3%)
    pallas_call x1, Pallas kernels, local(): pl.pallas_call(kernel, out_shape=pltpu.VMEM(features.shape, BF16), in_spe...  21.3 us
    unnamed x1, local copies, waits for them, and re-layouts  0.71 us

profile of v7, /device:TPU:192, one launch (start us, length us, event | category | flops | bytes accessed | tf_op | source)
XLA Modules:
  0.0 22.1 jit_solution(15871832444322769222)
XLA Ops:
  0.0 21.3 %conv_block.1 = bf16[2,8,64,128]{3,2,1,0:T(8,128)(2,1)S(1)} custom-call(bf16[2,8,64,128]{3,2,1,0:T(8,128)(2,1)} %refs_0_.1, bf16[3,3,3,128,128]{4,3,2,1,0:T(8,128)(2,1)} %refs_1_.1, bf16[3,3,3,128,128]{4,3,2,1,0:T(8,128)(2,1)} %refs_2_.1), custom_call_target="tpu_custom_call" | custom-call | flops 1811939328 | bytes 3145728 | tf_op jit(solution)/shard_map/conv_block/pallas_call | solution.py:548
  21.4 0.7 %copy.5 = bf16[2,8,64,128]{3,2,1,0:T(8,128)(2,1)} copy(bf16[2,8,64,128]{3,2,1,0:T(8,128)(2,1)S(1)} %conv_block.1) | data formatting | bytes 524288
